TPU v7x, 32 devices: a whole 2x2x4 slice. The times are simulated.
32 devices in a mesh: dp: 8 (over z, core), tensor: 4 (over y, x).
Axes of the slice: x: 2, y: 2, z: 4, core: 2. Of those that a mesh axis runs over, the one named last changes fastest.
Arguments:
- layer_input: bfloat16 [16, 1024, 1024], P('dp', 'tensor'), may hold values from -6 to 6
- memory: bfloat16 [16, 1024, 1024], P('dp', 'tensor'), may hold values from -6 to 6
- grad_out: bfloat16 [16, 1024, 1024], P('dp', 'tensor'), may hold values from -6 to 6
- target_segments: int32 [16, 1024], P('dp'), may hold values from 0 to 15, as said below
- source_segments: int32 [16, 1024], P('dp'), may hold values from 0 to 15, as said below
- self_gain: float32 [1024], replicated, may hold values from 0.5 to 1.5
- self_shift: float32 [1024], replicated, may hold values from -1.75 to 1.75
- query_weight: bfloat16 [1024, 1024], P(None, 'tensor'), may hold values from -0.1875 to 0.1875
- query_bias: float32 [1024], P('tensor'), may hold values from -1.75 to 1.75
- key_weight: bfloat16 [1024, 1024], P(None, 'tensor'), may hold values from -0.1875 to 0.1875
- value_weight: bfloat16 [1024, 1024], P(None, 'tensor'), may hold values from -0.1875 to 0.1875
- value_bias: float32 [1024], P('tensor'), may hold values from -1.75 to 1.75
- attend_weight: bfloat16 [1024, 1024], P('tensor'), may hold values from -0.5 to 0.5
- attend_bias: float32 [1024], replicated, may hold values from -1.75 to 1.75
- cross_gain: float32 [1024], replicated, may hold values from 0.5 to 1.5
- cross_shift: float32 [1024], replicated, may hold values from -1.75 to 1.75
- cross_query: bfloat16 [1024, 1024], P(None, 'tensor'), may hold values from -0.1875 to 0.1875
- cross_query_bias: float32 [1024], P('tensor'), may hold values from -1.75 to 1.75
- cross_key: bfloat16 [1024, 1024], P(None, 'tensor'), may hold values from -0.1875 to 0.1875
- cross_value: bfloat16 [1024, 1024], P(None, 'tensor'), may hold values from -0.1875 to 0.1875
- cross_value_bias: float32 [1024], P('tensor'), may hold values from -1.75 to 1.75
- cross_attend: bfloat16 [1024, 1024], P('tensor'), may hold values from -0.5 to 0.5
- cross_attend_bias: float32 [1024], replicated, may hold values from -1.75 to 1.75
- feed_gain: float32 [1024], replicated, may hold values from 0.5 to 1.5
- feed_shift: float32 [1024], replicated, may hold values from -1.75 to 1.75
- inner_weight: bfloat16 [1024, 4096], P(None, 'tensor'), may hold values from -0.1875 to 0.1875
- inner_bias: float32 [4096], P('tensor'), may hold values from -1.75 to 1.75
- outer_weight: bfloat16 [4096, 1024], P('tensor'), may hold values from -0.125 to 0.125
- outer_bias: float32 [1024], replicated, may hold values from -1.75 to 1.75
Outputs:
- block_out: bfloat16 [16, 1024, 1024], P('dp', 'tensor')
- input_grad: float32 [16, 1024, 1024], P('dp', 'tensor')
- memory_grad: float32 [16, 1024, 1024], P('dp', 'tensor')
- grad_self_gain: float32 [1024], replicated
- grad_self_shift: float32 [1024], replicated
- grad_query_weight: float32 [1024, 1024], P(None, 'tensor')
- grad_query_bias: float32 [1024], P('tensor')
- grad_key_weight: float32 [1024, 1024], P(None, 'tensor')
- grad_value_weight: float32 [1024, 1024], P(None, 'tensor')
- grad_value_bias: float32 [1024], P('tensor')
- grad_attend_weight: float32 [1024, 1024], P('tensor')
- grad_attend_bias: float32 [1024], replicated
- grad_cross_gain: float32 [1024], replicated
- grad_cross_shift: float32 [1024], replicated
- grad_cross_query: float32 [1024, 1024], P(None, 'tensor')
- grad_cross_query_bias: float32 [1024], P('tensor')
- grad_cross_key: float32 [1024, 1024], P(None, 'tensor')
- grad_cross_value: float32 [1024, 1024], P(None, 'tensor')
- grad_cross_value_bias: float32 [1024], P('tensor')
- grad_cross_attend: float32 [1024, 1024], P('tensor')
- grad_cross_attend_bias: float32 [1024], replicated
- grad_feed_gain: float32 [1024], replicated
- grad_feed_shift: float32 [1024], replicated
- grad_inner_weight: float32 [1024, 4096], P(None, 'tensor')
- grad_inner_bias: float32 [4096], P('tensor')
- grad_outer_weight: float32 [4096, 1024], P('tensor')
- grad_outer_bias: float32 [1024], replicated
Inputs may be any that keep to these rules, and one draw needn't show every extreme that they name: `target_segments`: in each row the ids never fall, start at 0 and every id from 0 to 15 appears. `source_segments`: in each row the ids never fall, start at 0 and every id from 0 to 15 appears, so each target pair has memory tokens of the same id in its row.
All inputs are finite; a program needn't handle non-finite values.
Results may differ from a plain program's by a relative error of at most 0.02.
Values may be sent and summed in bfloat16 or wider, within the bound.
A program may use at most 192 MiB of HBM per device.

v0:
```python
import jax
import jax.numpy as jnp
from jax import lax
from jax.sharding import PartitionSpec as P

HD = 64


EPSILON = 1e-05
MASKED = -1000000000.0
BLOCK_ROWS = 512


def norm_forward(values, gain, shift):
    average = jnp.mean(values, axis=-1, keepdims=True)
    center = values - average
    inverse = lax.rsqrt(jnp.mean(center * center, axis=-1, keepdims=True) + EPSILON)
    normed = center * inverse
    return ((normed * gain + shift).astype(jnp.bfloat16), normed, inverse)


def norm_backward(grad_in, normed, inverse, gain):
    scaled = grad_in * gain
    first_mean = jnp.mean(scaled, axis=-1, keepdims=True)
    second_mean = jnp.mean(scaled * normed, axis=-1, keepdims=True)
    grad_values = inverse * (scaled - first_mean - normed * second_mean)
    return (grad_values, jnp.sum(grad_in * normed, axis=(0, 1)), jnp.sum(grad_in, axis=(0, 1)))


def gather_rows(values):
    return lax.all_gather(values, "tensor", axis=1, tiled=True)


def gather_grads(values):
    return lax.all_gather(values, "tensor", axis=1, tiled=True)


def reduce_inputs(partial_sum):
    return lax.psum_scatter(partial_sum, "tensor", scatter_dimension=1, tiled=True)


def advance(base, partial_sum, bias):
    return base + lax.psum_scatter(partial_sum, "tensor", scatter_dimension=1, tiled=True) + bias


def next_rows(values, gain, shift):
    return gather_rows(norm_forward(values, gain, shift)[0])


def backward_rows(normed_low):
    return gather_rows(normed_low)


def project(rows_in, weight):
    return jnp.einsum("rtd,dc->rtc", rows_in, weight, preferred_element_type=jnp.float32)


def project_back(grads, weight):
    return jnp.einsum("rtc,dc->rtd", grads, weight, preferred_element_type=jnp.float32)


def outer_sum(rows_in, grads):
    return jnp.einsum("rtd,rtc->dc", rows_in, grads, preferred_element_type=jnp.float32)


def bias_sum(grads):
    return jnp.sum(grads.astype(jnp.float32), axis=(0, 1))


def split_heads(values):
    return values.reshape(values.shape[0], values.shape[1], values.shape[2] // HD, HD)


def block_scores(query_block, key_row, query_ids, key_ids, row_start, causal):
    raw_scores = jnp.einsum(
        "qhd,khd->hqk", query_block, key_row, preferred_element_type=jnp.float32
    ) * float(HD) ** (-0.5)
    allowed = query_ids[:, None] == key_ids[None, :]
    if causal:
        query_place = row_start + jnp.arange(query_block.shape[0], dtype=jnp.int32)
        key_place = jnp.arange(key_row.shape[0], dtype=jnp.int32)
        allowed = allowed & (key_place[None, :] <= query_place[:, None])
    return jnp.where(allowed[None], raw_scores, jnp.full(raw_scores.shape, MASKED, jnp.float32))


def block_inputs(
    query_heads, key_heads, value_heads, query_ids, key_ids, position, block_count, block_size
):
    row_index = position // block_count
    row_start = position % block_count * block_size
    query_row = lax.dynamic_index_in_dim(query_heads, row_index, 0, keepdims=False)
    query_block = lax.dynamic_slice_in_dim(query_row, row_start, block_size, 0)
    key_row = lax.dynamic_index_in_dim(key_heads, row_index, 0, keepdims=False)
    value_row = lax.dynamic_index_in_dim(value_heads, row_index, 0, keepdims=False)
    query_seg = lax.dynamic_slice_in_dim(
        lax.dynamic_index_in_dim(query_ids, row_index, 0, keepdims=False), row_start, block_size, 0
    )
    key_seg = lax.dynamic_index_in_dim(key_ids, row_index, 0, keepdims=False)
    return (row_index, row_start, query_block, key_row, value_row, query_seg, key_seg)


def attend_forward(query, keys, values, query_ids, key_ids, causal):
    query_heads = split_heads(query)
    key_heads = split_heads(keys)
    value_heads = split_heads(values)
    block_size = min(BLOCK_ROWS, query.shape[1])
    block_count = query.shape[1] // block_size

    def one_block(position):
        row_index, row_start, query_block, key_row, value_row, query_seg, key_seg = block_inputs(
            query_heads,
            key_heads,
            value_heads,
            query_ids,
            key_ids,
            position,
            block_count,
            block_size,
        )
        scores = block_scores(query_block, key_row, query_seg, key_seg, row_start, causal)
        row_max = jnp.max(scores, axis=-1, keepdims=True)
        expo_scores = jnp.exp(scores - row_max)
        row_total = jnp.sum(expo_scores, axis=-1, keepdims=True)
        softmax_out = expo_scores / row_total
        attended = jnp.einsum(
            "hqk,khd->qhd",
            softmax_out.astype(jnp.bfloat16),
            value_row,
            preferred_element_type=jnp.float32,
        ).astype(jnp.bfloat16)
        return (attended, (row_max + jnp.log(row_total))[..., 0])

    attended_all, log_sums = lax.map(
        one_block, jnp.arange(query.shape[0] * block_count, dtype=jnp.int32)
    )
    return (attended_all.reshape(query.shape), log_sums)


def attend_backward(query, keys, values, grad_att, log_sums, query_ids, key_ids, causal):
    query_heads = split_heads(query)
    key_heads = split_heads(keys)
    value_heads = split_heads(values)
    grad_heads = split_heads(grad_att)
    block_size = min(BLOCK_ROWS, query.shape[1])
    block_count = query.shape[1] // block_size
    score_scale = float(HD) ** (-0.5)

    def one_block(carry, inputs):
        grad_keys, grad_values = carry
        position, log_sum = inputs
        row_index, row_start, query_block, key_row, value_row, query_seg, key_seg = block_inputs(
            query_heads,
            key_heads,
            value_heads,
            query_ids,
            key_ids,
            position,
            block_count,
            block_size,
        )
        grad_row = lax.dynamic_index_in_dim(grad_heads, row_index, 0, keepdims=False)
        grad_block = lax.dynamic_slice_in_dim(grad_row, row_start, block_size, 0)
        scores = block_scores(query_block, key_row, query_seg, key_seg, row_start, causal)
        softmax_out = jnp.exp(scores - log_sum[..., None])
        softmax_low = softmax_out.astype(jnp.bfloat16)
        attended = jnp.einsum(
            "hqk,khd->qhd", softmax_low, value_row, preferred_element_type=jnp.float32
        ).astype(jnp.bfloat16)
        grad_prob = jnp.einsum(
            "qhd,khd->hqk", grad_block, value_row, preferred_element_type=jnp.float32
        )
        correction = jnp.sum(softmax_out * grad_prob, axis=-1, keepdims=True)
        grad_score = (softmax_out * (grad_prob - correction)).astype(jnp.bfloat16)
        grad_query = (
            jnp.einsum("hqk,khd->qhd", grad_score, key_row, preferred_element_type=jnp.float32)
            * score_scale
        ).astype(jnp.bfloat16)
        key_added = (
            jnp.einsum("hqk,qhd->khd", grad_score, query_block, preferred_element_type=jnp.float32)
            * score_scale
        )
        value_added = jnp.einsum(
            "hqk,qhd->khd", softmax_low, grad_block, preferred_element_type=jnp.float32
        )
        grad_keys = grad_keys.at[row_index].add(key_added)
        grad_values = grad_values.at[row_index].add(value_added)
        return ((grad_keys, grad_values), (grad_query, attended))

    empty_grads = jnp.zeros(key_heads.shape, jnp.float32)
    positions = jnp.arange(query.shape[0] * block_count, dtype=jnp.int32)
    (grad_keys, grad_values), (grad_query, attended_all) = lax.scan(
        one_block, (empty_grads, empty_grads), (positions, log_sums)
    )
    return (
        grad_query.reshape(query.shape),
        grad_keys.reshape(keys.shape).astype(jnp.bfloat16),
        grad_values.reshape(values.shape).astype(jnp.bfloat16),
        attended_all.reshape(query.shape),
    )


def local(
    layer_input,
    memory,
    grad_out,
    target_segments,
    source_segments,
    self_gain,
    self_shift,
    query_weight,
    query_bias,
    key_weight,
    value_weight,
    value_bias,
    attend_weight,
    attend_bias,
    cross_gain,
    cross_shift,
    cross_query,
    cross_query_bias,
    cross_key,
    cross_value,
    cross_value_bias,
    cross_attend,
    cross_attend_bias,
    feed_gain,
    feed_shift,
    inner_weight,
    inner_bias,
    outer_weight,
    outer_bias,
):
    inputs = layer_input.astype(jnp.float32)
    rows_first = next_rows(inputs, self_gain, self_shift)
    query_first = (project(rows_first, query_weight) + query_bias).astype(jnp.bfloat16)
    keys_first = project(rows_first, key_weight).astype(jnp.bfloat16)
    values_first = (project(rows_first, value_weight) + value_bias).astype(jnp.bfloat16)
    attended_first, sums_first = attend_forward(
        query_first, keys_first, values_first, target_segments, target_segments, True
    )
    base_first = advance(inputs, project(attended_first, attend_weight), attend_bias)
    memory_rows = lax.all_gather(memory, "tensor", axis=1, tiled=True)
    rows_second = next_rows(base_first, cross_gain, cross_shift)
    query_second = (project(rows_second, cross_query) + cross_query_bias).astype(jnp.bfloat16)
    keys_second = project(memory_rows, cross_key).astype(jnp.bfloat16)
    values_second = (project(memory_rows, cross_value) + cross_value_bias).astype(jnp.bfloat16)
    attended_second, sums_second = attend_forward(
        query_second, keys_second, values_second, target_segments, source_segments, False
    )
    base_second = advance(base_first, project(attended_second, cross_attend), cross_attend_bias)
    rows_third = next_rows(base_second, feed_gain, feed_shift)
    pre_active = project(rows_third, inner_weight) + inner_bias
    active = jax.nn.silu(pre_active).astype(jnp.bfloat16)
    base_out = advance(base_second, project(active, outer_weight), outer_bias)
    block_out = base_out.astype(jnp.bfloat16)
    kept_input, kept_first, kept_second, kept_memory, kept_sums_first, kept_sums_second = (
        lax.optimization_barrier(
            (inputs, base_first, base_second, memory_rows, sums_first, sums_second)
        )
    )
    grad_top = grad_out.astype(jnp.float32)
    normed_low3, unit_third, inverse_third = norm_forward(kept_second, feed_gain, feed_shift)
    rows_back3 = backward_rows(normed_low3)
    pre_back = project(rows_back3, inner_weight) + inner_bias
    sigmoid_back = jax.nn.sigmoid(pre_back)
    active_back = (pre_back * sigmoid_back).astype(jnp.bfloat16)
    grad_rows3 = gather_grads(grad_top.astype(jnp.bfloat16))
    grad_outer_weight = outer_sum(active_back, grad_rows3)
    grad_outer_bias = jnp.sum(grad_top, axis=(0, 1))
    grad_active = project_back(grad_rows3, outer_weight)
    grad_inner = (grad_active * sigmoid_back * (1.0 + pre_back * (1.0 - sigmoid_back))).astype(
        jnp.bfloat16
    )
    grad_inner_weight = outer_sum(rows_back3, grad_inner)
    grad_inner_bias = bias_sum(grad_inner)
    grad_norm3 = reduce_inputs(project_back(grad_inner, inner_weight))
    grad_from3, grad_feed_gain, grad_feed_shift = norm_backward(
        grad_norm3, unit_third, inverse_third, feed_gain
    )
    grad_hidden2 = grad_top + grad_from3
    normed_low2, unit_second, inverse_second = norm_forward(kept_first, cross_gain, cross_shift)
    rows_back2 = backward_rows(normed_low2)
    query_back2 = (project(rows_back2, cross_query) + cross_query_bias).astype(jnp.bfloat16)
    keys_back2 = project(kept_memory, cross_key).astype(jnp.bfloat16)
    values_back2 = (project(kept_memory, cross_value) + cross_value_bias).astype(jnp.bfloat16)
    grad_rows2 = gather_grads(grad_hidden2.astype(jnp.bfloat16))
    grad_att2 = project_back(grad_rows2, cross_attend).astype(jnp.bfloat16)
    grad_query2, grad_keys2, grad_values2, attended_back2 = attend_backward(
        query_back2,
        keys_back2,
        values_back2,
        grad_att2,
        kept_sums_second,
        target_segments,
        source_segments,
        False,
    )
    grad_cross_attend = outer_sum(attended_back2, grad_rows2)
    grad_cross_attend_bias = jnp.sum(grad_hidden2, axis=(0, 1))
    grad_cross_query = outer_sum(rows_back2, grad_query2)
    grad_cross_query_bias = bias_sum(grad_query2)
    grad_cross_key = outer_sum(kept_memory, grad_keys2)
    grad_cross_value = outer_sum(kept_memory, grad_values2)
    grad_cross_value_bias = bias_sum(grad_values2)
    memory_grad = lax.psum_scatter(
        (project_back(grad_keys2, cross_key) + project_back(grad_values2, cross_value)).astype(
            jnp.bfloat16
        ),
        "tensor",
        scatter_dimension=1,
        tiled=True,
    ).astype(jnp.float32)
    grad_norm2 = reduce_inputs(project_back(grad_query2, cross_query))
    grad_from2, grad_cross_gain, grad_cross_shift = norm_backward(
        grad_norm2, unit_second, inverse_second, cross_gain
    )
    grad_hidden1 = grad_hidden2 + grad_from2
    normed_low1, unit_first, inverse_first = norm_forward(kept_input, self_gain, self_shift)
    rows_back1 = backward_rows(normed_low1)
    query_back1 = (project(rows_back1, query_weight) + query_bias).astype(jnp.bfloat16)
    keys_back1 = project(rows_back1, key_weight).astype(jnp.bfloat16)
    values_back1 = (project(rows_back1, value_weight) + value_bias).astype(jnp.bfloat16)
    grad_rows1 = gather_grads(grad_hidden1.astype(jnp.bfloat16))
    grad_att1 = project_back(grad_rows1, attend_weight).astype(jnp.bfloat16)
    grad_query1, grad_keys1, grad_values1, attended_back1 = attend_backward(
        query_back1,
        keys_back1,
        values_back1,
        grad_att1,
        kept_sums_first,
        target_segments,
        target_segments,
        True,
    )
    grad_attend_weight = outer_sum(attended_back1, grad_rows1)
    grad_attend_bias = jnp.sum(grad_hidden1, axis=(0, 1))
    grad_query_weight = outer_sum(rows_back1, grad_query1)
    grad_query_bias = bias_sum(grad_query1)
    grad_key_weight = outer_sum(rows_back1, grad_keys1)
    grad_value_weight = outer_sum(rows_back1, grad_values1)
    grad_value_bias = bias_sum(grad_values1)
    grad_norm1 = reduce_inputs(
        project_back(grad_query1, query_weight)
        + project_back(grad_keys1, key_weight)
        + project_back(grad_values1, value_weight)
    )
    grad_from1, grad_self_gain, grad_self_shift = norm_backward(
        grad_norm1, unit_first, inverse_first, self_gain
    )
    input_grad = grad_hidden1 + grad_from1
    (
        grad_query_weight,
        grad_query_bias,
        grad_key_weight,
        grad_value_weight,
        grad_value_bias,
        grad_attend_weight,
        grad_cross_query,
        grad_cross_query_bias,
        grad_cross_key,
        grad_cross_value,
        grad_cross_value_bias,
        grad_cross_attend,
        grad_inner_weight,
        grad_inner_bias,
        grad_outer_weight,
    ) = (
        lax.psum(grad_query_weight.astype(jnp.bfloat16), "dp").astype(jnp.float32),
        lax.psum(grad_query_bias.astype(jnp.bfloat16), "dp").astype(jnp.float32),
        lax.psum(grad_key_weight.astype(jnp.bfloat16), "dp").astype(jnp.float32),
        lax.psum(grad_value_weight.astype(jnp.bfloat16), "dp").astype(jnp.float32),
        lax.psum(grad_value_bias.astype(jnp.bfloat16), "dp").astype(jnp.float32),
        lax.psum(grad_attend_weight.astype(jnp.bfloat16), "dp").astype(jnp.float32),
        lax.psum(grad_cross_query.astype(jnp.bfloat16), "dp").astype(jnp.float32),
        lax.psum(grad_cross_query_bias.astype(jnp.bfloat16), "dp").astype(jnp.float32),
        lax.psum(grad_cross_key.astype(jnp.bfloat16), "dp").astype(jnp.float32),
        lax.psum(grad_cross_value.astype(jnp.bfloat16), "dp").astype(jnp.float32),
        lax.psum(grad_cross_value_bias.astype(jnp.bfloat16), "dp").astype(jnp.float32),
        lax.psum(grad_cross_attend.astype(jnp.bfloat16), "dp").astype(jnp.float32),
        lax.psum(grad_inner_weight.astype(jnp.bfloat16), "dp").astype(jnp.float32),
        lax.psum(grad_inner_bias.astype(jnp.bfloat16), "dp").astype(jnp.float32),
        lax.psum(grad_outer_weight.astype(jnp.bfloat16), "dp").astype(jnp.float32),
    )
    (
        grad_self_gain,
        grad_self_shift,
        grad_attend_bias,
        grad_cross_gain,
        grad_cross_shift,
        grad_cross_attend_bias,
        grad_feed_gain,
        grad_feed_shift,
        grad_outer_bias,
    ) = lax.psum(
        (
            grad_self_gain,
            grad_self_shift,
            grad_attend_bias,
            grad_cross_gain,
            grad_cross_shift,
            grad_cross_attend_bias,
            grad_feed_gain,
            grad_feed_shift,
            grad_outer_bias,
        ),
        ("dp", "tensor"),
    )
    return (
        block_out,
        input_grad,
        memory_grad,
        grad_self_gain,
        grad_self_shift,
        grad_query_weight,
        grad_query_bias,
        grad_key_weight,
        grad_value_weight,
        grad_value_bias,
        grad_attend_weight,
        grad_attend_bias,
        grad_cross_gain,
        grad_cross_shift,
        grad_cross_query,
        grad_cross_query_bias,
        grad_cross_key,
        grad_cross_value,
        grad_cross_value_bias,
        grad_cross_attend,
        grad_cross_attend_bias,
        grad_feed_gain,
        grad_feed_shift,
        grad_inner_weight,
        grad_inner_bias,
        grad_outer_weight,
        grad_outer_bias,
    )


def solution(mesh):
    placed = (
        P("dp", "tensor", None),
        P("dp", "tensor", None),
        P("dp", "tensor", None),
        P("dp", None),
        P("dp", None),
        P(),
        P(),
        P(None, "tensor"),
        P("tensor"),
        P(None, "tensor"),
        P(None, "tensor"),
        P("tensor"),
        P("tensor", None),
        P(),
        P(),
        P(),
        P(None, "tensor"),
        P("tensor"),
        P(None, "tensor"),
        P(None, "tensor"),
        P("tensor"),
        P("tensor", None),
        P(),
        P(),
        P(),
        P(None, "tensor"),
        P("tensor"),
        P("tensor", None),
        P(),
    )
    return jax.shard_map(
        local,
        mesh=mesh,
        in_specs=placed,
        out_specs=(
            P("dp", "tensor", None),
            P("dp", "tensor", None),
            P("dp", "tensor", None),
            P(),
            P(),
            P(None, "tensor"),
            P("tensor"),
            P(None, "tensor"),
            P(None, "tensor"),
            P("tensor"),
            P("tensor", None),
            P(),
            P(),
            P(),
            P(None, "tensor"),
            P("tensor"),
            P(None, "tensor"),
            P(None, "tensor"),
            P("tensor"),
            P("tensor", None),
            P(),
            P(),
            P(),
            P(None, "tensor"),
            P("tensor"),
            P("tensor", None),
            P(),
        ),
        check_vma=False,
    )
```

profile of v0, /device:TPU:1, one launch (start us, length us, event | category | flops | bytes accessed | tf_op | source)
XLA Modules:
  0.0 1730.6 jit_solution(6767040679077723620)
XLA Ops:
  13.2 54.9 %all-gather.11.cloned.1.call-done = bf16[2,1024,1024]{2,1,0:T(8,128)(2,1)} async-done(((bf16[2,256,1024]{2,1,0:T(8,128)(2,1)}), bf16[2,1024,1024]{2,1,0:T(8,128)(2,1)}) %all-gather.11.cloned.1.call-update) | async-done | bytes 4194320 | tf_op jit(solution)/shard_map/all_gather | solution.py:31
  78.6 50.1 %while.72 = (s32[]{:T(128)}, bf16[4,512,4,64]{1,3,2,0:T(8,128)(2,1)}, f32[4,4,512]{2,1,0:T(4,128)S(1)}, s32[4]{0:T(128)S(1)}, bf16[2,1024,4,64]{1,3,2,0:T(8,128)...) while((s32[]{:T(128)}, ...), condition=%wide.region_5.6_spmd, body=%wide.region_2.5_spmd.sunk | while | flops 563739136 | bytes 33118724 | solution.py:133
  128.8 4.1 copy.157
  136.3 5.6 fusion.143
  143.1 85.4 %reduce-scatter.8.cloned.1.call-done = f32[2,256,1024]{2,1,0:T(8,128)} async-done(((f32[2,1024,1024]{2,1,0:T(8,128)}), f32[2,256,1024]{2,1,0:T(8,128)}) %reduce-scatter.8.cloned.1.call-update) | async-done | bytes 2097168 | tf_op jit(solution)/shard_map/reduce_scatter | solution.py:43
  233.1 50.0 %all-gather.13.cloned.1.call-done = bf16[2,1024,1024]{2,1,0:T(8,128)(2,1)} async-done(((bf16[2,256,1024]{2,1,0:T(8,128)(2,1)}), bf16[2,1024,1024]{2,1,0:T(8,128)(2,1)}) %all-gather.13.cloned.1.call-update) | async-done | bytes 4194320 | tf_op jit(solution)/shard_map/all_gather | solution.py:242
  283.2 4.7 convolution_convert_fusion.6
  290.2 48.1 %all-gather.15.cloned.1.call-done = bf16[2,1024,1024]{2,1,0:T(8,128)(2,1)} async-done(((bf16[2,256,1024]{2,1,0:T(8,128)(2,1)}), bf16[2,1024,1024]{2,1,0:T(8,128)(2,1)}) %all-gather.15.cloned.1.call-update) | async-done | bytes 4194320 | tf_op jit(solution)/shard_map/all_gather | solution.py:31
  338.4 4.6 add_convert_fusion.10
  344.0 49.8 %while.73 = (s32[]{:T(128)}, bf16[4,512,4,64]{1,3,2,0:T(8,128)(2,1)}, f32[4,4,512]{2,1,0:T(4,128)S(1)}, s32[4]{0:T(128)S(1)}, bf16[2,1024,4,64]{1,3,2,0:T(8,128)...) while((s32[]{:T(128)}, ...), condition=%wide.region_12.13_spmd, body=%wide.region_9.12_spmd.sunk | while | flops 562690048 | bytes 33114632 | solution.py:133
  393.8 4.1 copy.161
  397.9 4.3 reshape.767
  402.2 5.9 fusion.129
  409.9 84.8 %reduce-scatter.10.cloned.1.call-done = f32[2,256,1024]{2,1,0:T(8,128)} async-done(((f32[2,1024,1024]{2,1,0:T(8,128)}), f32[2,256,1024]{2,1,0:T(8,128)}) %reduce-scatter.10.cloned.1.call-update) | async-done | bytes 2097168 | tf_op jit(solution)/shard_map/reduce_scatter | solution.py:43
  507.2 52.1 %all-gather.21.cloned.1.call-done = bf16[2,1024,1024]{2,1,0:T(8,128)(2,1)} async-done(((bf16[2,256,1024]{2,1,0:T(8,128)(2,1)}), bf16[2,1024,1024]{2,1,0:T(8,128)(2,1)}) %all-gather.21.cloned.1.call-update) | async-done | bytes 4194320 | tf_op jit(solution)/shard_map/all_gather | solution.py:31
  559.3 9.0 fusion.114
  568.3 45.6 %all-gather.19.cloned.1.call-done = bf16[2,1024,1024]{2,1,0:T(8,128)(2,1)} async-done(((bf16[2,256,1024]{2,1,0:T(8,128)(2,1)}), bf16[2,1024,1024]{2,1,0:T(8,128)(2,1)}) %all-gather.19.cloned.1.call-update) | async-done | bytes 4194320 | tf_op jit(solution)/shard_map/all_gather | solution.py:35
  613.8 10.9 fusion.164
  626.7 6.9 fusion.112
  640.9 79.3 %reduce-scatter.14.cloned.1.call-done = f32[2,256,1024]{2,1,0:T(8,128)} async-done(((f32[2,1024,1024]{2,1,0:T(8,128)}), f32[2,256,1024]{2,1,0:T(8,128)}) %reduce-scatter.14.cloned.1.call-update) | async-done | bytes 2097168 | tf_op jit(solution)/shard_map/reduce_scatter | solution.py:39
  720.2 4.0 multiply_reduce_fusion.2
  728.3 4.2 convolution_convert_fusion.5
  736.0 39.6 %all-gather.23.cloned.1.call-done = bf16[2,1024,1024]{2,1,0:T(8,128)(2,1)} async-done(((bf16[2,256,1024]{2,1,0:T(8,128)(2,1)}), bf16[2,1024,1024]{2,1,0:T(8,128)(2,1)}) %all-gather.23.cloned.1.call-update) | async-done | bytes 4194320 | tf_op jit(solution)/shard_map/all_gather | solution.py:31
  775.6 4.6 add_convert_fusion.5
  780.1 50.6 %all-gather.25.cloned.1.call-done = bf16[2,1024,1024]{2,1,0:T(8,128)(2,1)} async-done(((bf16[2,256,1024]{2,1,0:T(8,128)(2,1)}), bf16[2,1024,1024]{2,1,0:T(8,128)(2,1)}) %all-gather.25.cloned.1.call-update) | async-done | bytes 4194320 | tf_op jit(solution)/shard_map/all_gather | solution.py:35
  830.7 4.6 convolution_convert_fusion.4
  840.6 100.2 %while.74 = (s32[]{:T(128)}, f32[2,1024,4,64]{1,3,2,0:T(8,128)}, f32[2,1024,4,64]{1,3,2,0:T(8,128)}, bf16[4,512,4,64]{1,3,2,0:T(8,128)(2,1)}, bf16[4,512,4,64]{1...) while((s32[]{:T(128)}, f32[2,1024,4,64]{1,3,2,0:T(8,128)}, ...), condition=%wide.region_27.28_spmd, body=%wide.region_24.27_spmd.sunk | while | flops 1652684800 | bytes 123819264 | solution.py:191
  940.8 4.1 copy.170
  948.5 5.9 fusion.135
  961.9 79.1 %reduce-scatter.16.cloned.1.call-done = f32[2,256,1024]{2,1,0:T(8,128)} async-done(((f32[2,1024,1024]{2,1,0:T(8,128)}), f32[2,256,1024]{2,1,0:T(8,128)}) %reduce-scatter.16.cloned.1.call-update) | async-done | bytes 2097168 | tf_op jit(solution)/shard_map/reduce_scatter | solution.py:39
  1050.5 45.6 %all-gather.17.cloned.1.call-done = bf16[2,1024,1024]{2,1,0:T(8,128)(2,1)} async-done(((bf16[2,256,1024]{2,1,0:T(8,128)(2,1)}), bf16[2,1024,1024]{2,1,0:T(8,128)(2,1)}) %all-gather.17.cloned.1.call-update) | async-done | bytes 4194320 | tf_op jit(solution)/shard_map/all_gather | solution.py:31
  1096.0 13.2 fusion.106
  1109.3 41.9 %all-gather.27.cloned.1.call-done = bf16[2,1024,1024]{2,1,0:T(8,128)(2,1)} async-done(((bf16[2,256,1024]{2,1,0:T(8,128)(2,1)}), bf16[2,1024,1024]{2,1,0:T(8,128)(2,1)}) %all-gather.27.cloned.1.call-update) | async-done | bytes 4194320 | tf_op jit(solution)/shard_map/all_gather | solution.py:31
  1151.2 4.6 add_convert_fusion.1
  1160.5 10.7 bitcast_convert_fusion
  1171.2 5.8 bitcast_convert_fusion.1
  1184.3 4.7 fusion.123
  1193.8 12.4 all-gather.29.cloned.1.call-done
  1206.2 4.6 convolution_convert_fusion.2
  1216.1 103.8 %while.75 = (s32[]{:T(128)}, f32[2,1024,4,64]{1,3,2,0:T(8,128)}, f32[2,1024,4,64]{1,3,2,0:T(8,128)}, bf16[4,512,4,64]{1,3,2,0:T(8,128)(2,1)}, bf16[4,512,4,64]{1...) while((s32[]{:T(128)}, f32[2,1024,4,64]{1,3,2,0:T(8,128)}, ...), condition=%wide.region_36.37_spmd, body=%wide.region_33.36_spmd.sunk | while | flops 1653733888 | bytes 123823352 | solution.py:191
  1329.3 4.3 reshape.769
  1361.3 4.6 add_add_fusion
  1372.4 14.6 all-reduce.1
  1389.9 139.6 %all-reduce.5.cloned.1.call-done = (bf16[1024,256]{1,0:T(8,128)(2,1)}, bf16[1024,256]{1,0:T(8,128)(2,1)}, bf16[1024,256]{1,0:T(8,128)(2,1)}, bf16[256,1024]{1,0:...) async-done(((bf16[1024,256]{1,0:T(8,128)(2,1)}, ...) | async-done | bytes 8388624 | tf_op jit(solution)/shard_map/psum | solution.py:368
  1546.3 39.6 %reduce-scatter.20.cloned.1.call-done = bf16[2,256,1024]{2,1,0:T(8,128)(2,1)} async-done(((bf16[2,1024,1024]{2,1,0:T(8,128)(2,1)}), bf16[2,256,1024]{2,1,0:T(8,128)(2,1)}) %reduce-scatter.20.cloned.1.call-update) | async-done | bytes 1048592 | tf_op jit(solution)/shard_map/reduce_scatter | solution.py:305
  1588.7 86.5 %reduce-scatter.18.cloned.1.call-done = f32[2,256,1024]{2,1,0:T(8,128)} async-done(((f32[2,1024,1024]{2,1,0:T(8,128)}), f32[2,256,1024]{2,1,0:T(8,128)}) %reduce-scatter.18.cloned.1.call-update) | async-done | bytes 2097168 | tf_op jit(solution)/shard_map/reduce_scatter | solution.py:39
  1678.6 39.9 %all-reduce = (f32[1024]{0:T(1024)}, f32[1024]{0:T(1024)}, f32[1024]{0:T(1024)}, f32[1024]{0:T(1024)}, f32[1024]{0:T(1024)}, /*index=5*/f32[1024]{0:T(1024)}, f32[1024]{0:T(1024)}, f32[1024]{0:T(1024)}, f32[1024]{0:T(1024)}) all-reduce(f32[1024]{0:T(1024)S(1)} %get-tuple-element.803, ...), channel_id=1, replica_groups=mesh['dp'=8,'tensor'=4] {'dp','tensor'}, use_global_device_ids=true, to_apply=%region_42.43 | all-reduce | flops 9216 | bytes 73728 | tf_op jit(solution)/shard_map/psum | solution.py:394
  1718.4 4.8 multiply_add_fusion
  (616 shorter events, 437.2 us)
Async XLA Ops:
  7.2 552.1 %copy-start = (bf16[1024,1024]{1,0:T(8,128)(2,1)S(1)}, bf16[1024,1024]{1,0:T(8,128)(2,1)}, u32[]{:S(2)}) copy-start(bf16[1024,1024]{1,0:T(8,128)(2,1)} %param.70) | copy-start | bytes 6291460
  7.2 60.9 %all-gather.11.cloned.1.call-start = ((), (), s32[]{:S(2)}) async-start(), calls=%async_computation.7 | async-start | bytes 5242880 | tf_op jit(solution)/shard_map/all_gather | solution.py:31
  13.2 58.7 %copy-start.99 = (f32[256]{0:T(256)S(1)}, f32[256]{0:T(256)}, u32[]{:S(2)}) copy-start(f32[256]{0:T(256)} %param.53) | copy-start | bytes 3076
  13.2 215.2 %reduce-scatter.8.cloned.1.call-start = ((), (), s32[]{:S(2)}) async-start(), calls=%async_computation.8 | async-start | bytes 10485760 | tf_op jit(solution)/shard_map/reduce_scatter | solution.py:43
  128.8 13.1 copy-start.54
  141.9 86.6 %copy-start.9 = (bf16[2,256,1024]{2,1,0:T(8,128)(2,1)S(1)}, bf16[2,256,1024]{2,1,0:T(8,128)(2,1)}, u32[]{:S(2)}) copy-start(bf16[2,256,1024]{2,1,0:T(8,128)(2,1)} %param.45) | copy-start | bytes 3145732
  141.9 86.6 %copy-start.76 = (f32[1024]{0:T(1024)S(1)}, f32[1024]{0:T(1024)}, u32[]{:S(2)}) copy-start(f32[1024]{0:T(1024)} %param.58) | copy-start | bytes 12292
  141.9 89.8 %copy-start.55 = (f32[1024]{0:T(1024)S(1)}, f32[1024]{0:T(1024)}, u32[]{:S(2)}) copy-start(f32[1024]{0:T(1024)} %param.59) | copy-start | bytes 12292
  141.9 89.8 %copy-start.65 = (f32[1024]{0:T(1024)S(1)}, f32[1024]{0:T(1024)}, u32[]{:S(2)}) copy-start(f32[1024]{0:T(1024)} %param.60) | copy-start | bytes 12292
  141.9 141.3 %all-gather.13.cloned.1.call-start = ((), (), s32[]{:S(2)}) async-start(), calls=%async_computation.9 | async-start | bytes 5242880 | tf_op jit(solution)/shard_map/all_gather | solution.py:242
  142.7 195.7 %all-gather.15.cloned.1.call-start = ((), (), s32[]{:S(2)}) async-start(), calls=%async_computation.10 | async-start | bytes 5242880 | tf_op jit(solution)/shard_map/all_gather | solution.py:31
  233.1 54.9 %copy-start.93 = (f32[256]{0:T(256)S(1)}, f32[256]{0:T(256)}, u32[]{:S(2)}) copy-start(f32[256]{0:T(256)} %param.65) | copy-start | bytes 3076
  233.1 261.6 %reduce-scatter.10.cloned.1.call-start = ((), (), s32[]{:S(2)}) async-start(), calls=%async_computation.11 | async-start | bytes 10485760 | tf_op jit(solution)/shard_map/reduce_scatter | solution.py:43
  287.9 50.4 %copy-start.95 = (f32[256]{0:T(256)S(1)}, f32[256]{0:T(256)}, u32[]{:S(2)}) copy-start(f32[256]{0:T(256)} %param.62) | copy-start | bytes 3076
  290.2 53.8 %copy-start.53 = (s32[2,1024]{1,0:T(2,128)S(1)}, s32[2,1024]{1,0:T(2,128)}, u32[]{:S(2)}) copy-start(s32[2,1024]{1,0:T(2,128)} %param.49) | copy-start | bytes 24580
  408.1 86.5 %copy-start.75 = (f32[1024]{0:T(1024)S(1)}, f32[1024]{0:T(1024)}, u32[]{:S(2)}) copy-start(f32[1024]{0:T(1024)} %param.67) | copy-start | bytes 12292
  408.1 151.1 %all-gather.21.cloned.1.call-start = ((), (), s32[]{:S(2)}) async-start(), calls=%async_computation.15 | async-start | bytes 5242880 | tf_op jit(solution)/shard_map/all_gather | solution.py:31
  506.4 107.5 %all-gather.19.cloned.1.call-start = ((), (), s32[]{:S(2)}) async-start(), calls=%async_computation.14 | async-start | bytes 5242880 | tf_op jit(solution)/shard_map/all_gather | solution.py:35
  507.1 106.7 %copy-start.91 = (f32[1024]{0:T(1024)S(1)}, f32[1024]{0:T(1024)}, u32[]{:S(2)}) copy-start(f32[1024]{0:T(1024)} %param.71) | copy-start | bytes 12292
  507.1 213.1 %reduce-scatter.14.cloned.1.call-start = ((), (), s32[]{:S(2)}) async-start(), calls=%async_computation.16 | async-start | bytes 10485760 | tf_op jit(solution)/shard_map/reduce_scatter | solution.py:39
  633.7 141.8 %all-gather.23.cloned.1.call-start = ((), (), s32[]{:S(2)}) async-start(), calls=%async_computation.17 | async-start | bytes 5242880 | tf_op jit(solution)/shard_map/all_gather | solution.py:31
  637.5 86.7 %copy-start.28 = (bf16[2,256,1024]{2,1,0:T(8,128)(2,1)S(1)}, bf16[2,256,1024]{2,1,0:T(8,128)(2,1)}, u32[]{:S(2)}) copy-start(bf16[2,256,1024]{2,1,0:T(8,128)(2,1)} %param.47) | copy-start | bytes 3145732
  640.6 190.1 %all-gather.25.cloned.1.call-start = ((), (), s32[]{:S(2)}) async-start(), calls=%async_computation.18 | async-start | bytes 5242880 | tf_op jit(solution)/shard_map/all_gather | solution.py:35
  728.2 312.8 %reduce-scatter.16.cloned.1.call-start = ((), (), s32[]{:S(2)}) async-start(), calls=%async_computation.19 | async-start | bytes 10485760 | tf_op jit(solution)/shard_map/reduce_scatter | solution.py:39
  732.7 42.9 %copy-start.96 = (f32[256]{0:T(256)S(1)}, f32[256]{0:T(256)}, u32[]{:S(2)}) copy-start(f32[256]{0:T(256)} %param.62) | copy-start | bytes 3076
  954.5 141.5 %all-gather.17.cloned.1.call-start = ((), (), s32[]{:S(2)}) async-start(), calls=%async_computation.12 | async-start | bytes 5242880 | tf_op jit(solution)/shard_map/all_gather | solution.py:31
  955.1 196.1 %all-gather.27.cloned.1.call-start = ((), (), s32[]{:S(2)}) async-start(), calls=%async_computation.20 | async-start | bytes 5242880 | tf_op jit(solution)/shard_map/all_gather | solution.py:31
  956.9 88.1 %copy-start.59 = (f32[2,256]{1,0:T(2,128)}, f32[2,256]{1,0:T(2,128)S(1)}, u32[]{:S(2)}) copy-start(f32[2,256]{1,0:T(2,128)S(1)} %broadcast_multiply_fusion.2) | copy-start | bytes 6148
  958.9 86.1 %copy-start.63 = (f32[2,256]{1,0:T(2,128)}, f32[2,256]{1,0:T(2,128)S(1)}, u32[]{:S(2)}) copy-start(f32[2,256]{1,0:T(2,128)S(1)} %add_rsqrt_fusion) | copy-start | bytes 6148
  961.9 244.3 %all-gather.29.cloned.1.call-start = ((), (), s32[]{:S(2)}) async-start(), calls=%async_computation.21 | async-start | bytes 5242880 | tf_op jit(solution)/shard_map/all_gather | solution.py:35
  1047.9 48.1 %copy-start.92 = (f32[1024]{0:T(1024)S(1)}, f32[1024]{0:T(1024)}, u32[]{:S(2)}) copy-start(f32[1024]{0:T(1024)} %param.71) | copy-start | bytes 12292
  1050.4 315.6 %reduce-scatter.12.cloned.1.call-start = ((), (), s32[]{:S(2)}) async-start(), calls=%async_computation.13 | async-start | bytes 10485760 | tf_op jit(solution)/shard_map/reduce_scatter | solution.py:43
  1109.3 41.9 %copy-start.46 = (bf16[1024,256]{1,0:T(8,128)(2,1)S(1)}, bf16[1024,256]{1,0:T(8,128)(2,1)}, u32[]{:S(2)}) copy-start(bf16[1024,256]{1,0:T(8,128)(2,1)} %param.55) | copy-start | bytes 1572868
  1109.3 41.9 %copy-start.98 = (f32[256]{0:T(256)S(1)}, f32[256]{0:T(256)}, u32[]{:S(2)}) copy-start(f32[256]{0:T(256)} %param.56) | copy-start | bytes 3076
  1109.3 420.1 %all-reduce.5.cloned.1.call-start = ((), (), s32[]{:S(2)}) async-start(), calls=%async_computation.24 | async-start | bytes 16777216 | tf_op jit(solution)/shard_map/psum | solution.py:368
  1160.5 10.7 copy-start.104
  1350.5 235.4 %reduce-scatter.20.cloned.1.call-start = ((), (), s32[]{:S(2)}) async-start(), calls=%async_computation.23 | async-start | bytes 5242880 | tf_op jit(solution)/shard_map/reduce_scatter | solution.py:305
  1357.0 318.2 %reduce-scatter.18.cloned.1.call-start = ((), (), s32[]{:S(2)}) async-start(), calls=%async_computation.22 | async-start | bytes 10485760 | tf_op jit(solution)/shard_map/reduce_scatter | solution.py:39
  1543.8 131.5 %copy-start.58 = (f32[1024]{0:T(1024)S(1)}, f32[1024]{0:T(1024)}, u32[]{:S(2)}) copy-start(f32[1024]{0:T(1024)} %param.50) | copy-start | bytes 12292
  1543.8 131.5 %copy-start.60 = (f32[2,256]{1,0:T(2,128)S(1)}, f32[2,256]{1,0:T(2,128)}, u32[]{:S(2)}) copy-start(f32[2,256]{1,0:T(2,128)} %copy-done.59) | copy-start | bytes 6148
  1543.8 131.5 %copy-start.64 = (f32[2,256]{1,0:T(2,128)S(1)}, f32[2,256]{1,0:T(2,128)}, u32[]{:S(2)}) copy-start(f32[2,256]{1,0:T(2,128)} %copy-done.63) | copy-start | bytes 6148
  1546.2 132.3 %copy-start.68 = (f32[1024]{0:T(1024)S(1)}, f32[1024]{0:T(1024)}, u32[]{:S(2)}) copy-start(f32[1024]{0:T(1024)} %get-tuple-element.799) | copy-start | bytes 12292
  1546.2 132.3 %copy-start.69 = (f32[1024]{0:T(1024)S(1)}, f32[1024]{0:T(1024)}, u32[]{:S(2)}) copy-start(f32[1024]{0:T(1024)} %get-tuple-element.808) | copy-start | bytes 12292
  1546.2 132.3 %copy-start.70 = (f32[1024]{0:T(1024)S(1)}, f32[1024]{0:T(1024)}, u32[]{:S(2)}) copy-start(f32[1024]{0:T(1024)} %get-tuple-element.923) | copy-start | bytes 12292
  1546.3 132.3 %copy-start.71 = (f32[1024]{0:T(1024)S(1)}, f32[1024]{0:T(1024)}, u32[]{:S(2)}) copy-start(f32[1024]{0:T(1024)} %get-tuple-element.939) | copy-start | bytes 12292
  1546.3 132.3 %copy-start.72 = (f32[1024]{0:T(1024)S(1)}, f32[1024]{0:T(1024)}, u32[]{:S(2)}) copy-start(f32[1024]{0:T(1024)} %get-tuple-element.801) | copy-start | bytes 12292
  1546.3 132.3 %copy-start.73 = (f32[1024]{0:T(1024)S(1)}, f32[1024]{0:T(1024)}, u32[]{:S(2)}) copy-start(f32[1024]{0:T(1024)} %get-tuple-element.809) | copy-start | bytes 12292
  1546.3 132.3 %copy-start.74 = (f32[1024]{0:T(1024)S(1)}, f32[1024]{0:T(1024)}, u32[]{:S(2)}) copy-start(f32[1024]{0:T(1024)} %get-tuple-element.925) | copy-start | bytes 12292
  (117 other events, 401.4 us)
Sparse Core Ops, SparseCore 0:
  13.3 54.7 all-gather.10
  142.0 86.3 reduce-scatter.7
  230.4 52.7 all-gather.12
  285.6 52.6 all-gather.14
  408.3 86.3 reduce-scatter.9
  506.5 52.7 all-gather.20
  561.1 52.6 all-gather.18
  633.8 86.3 reduce-scatter.13
  722.8 52.7 all-gather.22
  778.0 52.6 all-gather.24
  954.6 86.3 reduce-scatter.15
  1043.3 52.7 all-gather.16
  1098.5 52.6 all-gather.26
  1153.5 52.6 all-gather.28
  1209.1 86.3 reduce-scatter.11
  1350.6 178.7 all-reduce.4
  1532.5 53.3 reduce-scatter.19
  1588.9 86.3 reduce-scatter.17
where the time goes:
time: 1740 us; the launch traced here: 1730 us
  waiting for transfers between devices  1040 us (60%)
  matrix products  345 us (20%)
  other arithmetic  144 us (8%)
  local copies, waits for them, and re-layouts  89.4 us (5%)
  blocking collectives  54.4 us (3%)
  loops' own time  43.7 us (3%)
    all_gather x6, waiting for transfers between devices, gather_rows(): return lax.all_gather(values, 'tensor', axis=1, tiled=True)  282 us
    reduce_scatter x3, waiting for transfers between devices, reduce_inputs(): lax.psum_scatter(partial_sum, 'tensor', scatter_dimension=1, tiled=True)  245 us
    reduce_scatter x3, waiting for transfers between devices, advance(): lax.psum_scatter(partial_sum, 'tensor', scatter_dimension=1, tiled=True)  170 us
    psum x1, waiting for transfers between devices, local(): lax.psum(grad_query_weight.astype(jnp.bfloat16), 'dp').astype(jnp.float32)  140 us
    all_gather x3, waiting for transfers between devices, gather_grads(): return lax.all_gather(values, 'tensor', axis=1, tiled=True)  109 us
    dot_general x16, matrix products, project(): jnp.einsum('rtd,dc->rtc', rows_in, weight, preferred_element_type=jnp.flo...  76 us
    all_gather x1, waiting for transfers between devices, local(): memory_rows = lax.all_gather(memory, 'tensor', axis=1, tiled=True)  50 us
    dot_general x10, matrix products, project_back(): jnp.einsum('rtc,dc->rtd', grads, weight, preferred_element_type=jnp.float32)  47.8 us
  transfers between devices with their start and end apart: 18, of which 17 were waited for; matrix products, arithmetic and copies ran while one was open for 17% of the time, Pallas kernels for 0%

commit v1 on v0

--- a/solution.py
+++ b/solution.py
@@ -1,17 +1,597 @@
 import jax
 import jax.numpy as jnp
 from jax import lax
+from jax.experimental import pallas as pl
+from jax.experimental.pallas import tpu as pltpu
 from jax.sharding import PartitionSpec as P
 
 HD = 64
+MASKED = -1000000000.0
+QUERIES = 128
+KEYS = 256
+NT = (((1,), (1,)), ((), ()))
+TN = (((0,), (0,)), ((), ()))
+NN = (((1,), (0,)), ((), ()))
+
+
+def dot(a, b, dims):
+    return lax.dot_general(a, b, dims, preferred_element_type=jnp.float32)
+
+
+def both_heads(block):
+    first = lax.broadcasted_iota(jnp.int32, block.shape, 1) < HD
+    zero = jnp.zeros_like(block)
+    return jnp.concatenate([jnp.where(first, block, zero), jnp.where(first, zero, block)], axis=0)
+
+
+def key_span(bounds, place, count, step):
+    start = bounds[0, place] + step * KEYS
+    at = pl.multiple_of(jnp.minimum(start, count - KEYS), 16)
+    return start, at
+
+
+def allowed_keys(low_ref, high_ref, start, at):
+    key_place = at + lax.broadcasted_iota(jnp.int32, (KEYS, 1), 0)
+    least = jnp.maximum(low_ref[...], start)
+    seen = (key_place >= least) & (key_place < high_ref[...])
+    return jnp.concatenate([seen, seen], axis=1)
+
+
+def attend_kernel(bounds, low_ref, high_ref, q_ref, k_ref, v_ref, out_ref, sums_ref, acc, top, total):
+    pairs = q_ref.shape[1] // 128
+    count = k_ref.shape[0]
+    place = pl.program_id(0)
+    acc[...] = jnp.zeros_like(acc)
+    total[...] = jnp.zeros_like(total)
+    top[...] = jnp.full_like(top, -1e30)
+    queries = [both_heads(q_ref[:, p * 128:(p + 1) * 128] * jnp.bfloat16(HD ** -0.5)) for p in range(pairs)]
+
+    def step(j, _):
+        start, at = key_span(bounds, place, count, j)
+        seen = allowed_keys(low_ref, high_ref, start, at)
+        for p in range(pairs):
+            keys = k_ref[pl.ds(at, KEYS), p * 128:(p + 1) * 128]
+            values = v_ref[pl.ds(at, KEYS), p * 128:(p + 1) * 128]
+            scores = jnp.where(seen, dot(keys, queries[p], NT), MASKED)
+            before = top[p:p + 1]
+            now = jnp.maximum(before, jnp.max(scores, axis=0, keepdims=True))
+            weight = jnp.exp(scores - now)
+            keep = jnp.exp(before - now)
+            top[p:p + 1] = now
+            total[p:p + 1] = total[p:p + 1] * keep + jnp.sum(weight, axis=0, keepdims=True)
+            acc[p] = acc[p] * keep + dot(values, weight.astype(jnp.bfloat16), TN)
+        return 0
+
+    lax.fori_loop(0, bounds[1, place], step, 0)
+    for p in range(pairs):
+        sums = total[p:p + 1]
+        mixed = acc[p] / sums
+        joined = jnp.concatenate([mixed[:HD, :QUERIES], mixed[HD:, QUERIES:]], axis=0)
+        out_ref[:, p * 128:(p + 1) * 128] = joined.T.astype(jnp.bfloat16)
+        sums_ref[p:p + 1] = top[p:p + 1] + jnp.log(sums)
+
+
+def attend(q, k, v, bounds, low, high):
+    count, width = q.shape
+    source = k.shape[0]
+    pairs = width // 128
+    whole = lambda i, b: (0, 0)
+    return pl.pallas_call(
+        attend_kernel,
+        grid_spec=pltpu.PrefetchScalarGridSpec(
+            num_scalar_prefetch=1,
+            grid=(count // QUERIES,),
+            in_specs=[
+                pl.BlockSpec((1, QUERIES), lambda i, b: (0, i)),
+                pl.BlockSpec((1, QUERIES), lambda i, b: (0, i)),
+                pl.BlockSpec((QUERIES, width), lambda i, b: (i, 0)),
+                pl.BlockSpec((source, width), whole),
+                pl.BlockSpec((source, width), whole),
+            ],
+            out_specs=[
+                pl.BlockSpec((QUERIES, width), lambda i, b: (i, 0)),
+                pl.BlockSpec((None, pairs, 2 * QUERIES), lambda i, b: (i, 0, 0)),
+            ],
+            scratch_shapes=[
+                pltpu.VMEM((pairs, 128, 2 * QUERIES), jnp.float32),
+                pltpu.VMEM((pairs, 2 * QUERIES), jnp.float32),
+                pltpu.VMEM((pairs, 2 * QUERIES), jnp.float32),
+            ],
+        ),
+        out_shape=[
+            jax.ShapeDtypeStruct((count, width), jnp.bfloat16),
+            jax.ShapeDtypeStruct((count // QUERIES, pairs, 2 * QUERIES), jnp.float32),
+        ],
+        compiler_params=pltpu.CompilerParams(vmem_limit_bytes=32 << 20),
+        cost_estimate=pl.CostEstimate(flops=4 * count * 400 * width, bytes_accessed=8 * count * width, transcendentals=0),
+        name="attend",
+    )(bounds, low, high, q, k, v)
+
+
+def attend_back_kernel(
+    bounds, low_ref, high_ref, q_ref, grad_ref, out_ref, sums_ref, k_ref, v_ref,
+    dq_ref, dk_ref, dv_ref, acc, acc_k, acc_v,
+):
+    pairs = q_ref.shape[1] // 128
+    count = k_ref.shape[0]
+    place = pl.program_id(0)
+
+    @pl.when(place == 0)
+    def _():
+        acc_k[...] = jnp.zeros_like(acc_k)
+        acc_v[...] = jnp.zeros_like(acc_v)
+
+    acc[...] = jnp.zeros_like(acc)
+    queries, grads, fixes = [], [], []
+    ones = jnp.ones((8, 128), jnp.bfloat16)
+    for p in range(pairs):
+        cut = slice(p * 128, (p + 1) * 128)
+        queries.append(both_heads(q_ref[:, cut] * jnp.bfloat16(HD ** -0.5)))
+        grad = both_heads(grad_ref[:, cut])
+        grads.append(grad)
+        out = out_ref[:, cut].astype(jnp.float32)
+        product = grad.astype(jnp.float32) * jnp.concatenate([out, out], axis=0)
+        coarse = product.astype(jnp.bfloat16)
+        fine = (product - coarse.astype(jnp.float32)).astype(jnp.bfloat16)
+        fixes.append((dot(ones, coarse, NT) + dot(ones, fine, NT))[:1])
+
+    def step(j, _):
+        start, at = key_span(bounds, place, count, j)
+        seen = allowed_keys(low_ref, high_ref, start, at)
+        rows = pl.ds(at, KEYS)
+        for p in range(pairs):
+            cut = slice(p * 128, (p + 1) * 128)
+            keys = k_ref[rows, cut]
+            values = v_ref[rows, cut]
+            scores = dot(keys, queries[p], NT)
+            prob = jnp.exp(jnp.where(seen, scores - sums_ref[p:p + 1], MASKED))
+            dprob = dot(values, grads[p], NT)
+            dscore = (prob * (dprob - fixes[p])).astype(jnp.bfloat16)
+            acc_v[rows, cut] += dot(prob.astype(jnp.bfloat16), grads[p], NN)
+            acc_k[rows, cut] += dot(dscore, queries[p], NN)
+            acc[p] += dot(keys, dscore, TN)
+        return 0
+
+    lax.fori_loop(0, bounds[1, place], step, 0)
+    for p in range(pairs):
+        mixed = acc[p] * (HD ** -0.5)
+        joined = jnp.concatenate([mixed[:HD, :QUERIES], mixed[HD:, QUERIES:]], axis=0)
+        dq_ref[:, p * 128:(p + 1) * 128] = joined.T.astype(jnp.bfloat16)
+
+    @pl.when(place == pl.num_programs(0) - 1)
+    def _():
+        dk_ref[...] = acc_k[...].astype(jnp.bfloat16)
+        dv_ref[...] = acc_v[...].astype(jnp.bfloat16)
+
+
+def attend_back(q, k, v, grad, out, sums, bounds, low, high):
+    count, width = q.shape
+    source = k.shape[0]
+    pairs = width // 128
+    whole = lambda i, b: (0, 0)
+    rows = lambda i, b: (i, 0)
+    return pl.pallas_call(
+        attend_back_kernel,
+        grid_spec=pltpu.PrefetchScalarGridSpec(
+            num_scalar_prefetch=1,
+            grid=(count // QUERIES,),
+            in_specs=[
+                pl.BlockSpec((1, QUERIES), lambda i, b: (0, i)),
+                pl.BlockSpec((1, QUERIES), lambda i, b: (0, i)),
+                pl.BlockSpec((QUERIES, width), rows),
+                pl.BlockSpec((QUERIES, width), rows),
+                pl.BlockSpec((QUERIES, width), rows),
+                pl.BlockSpec((None, pairs, 2 * QUERIES), lambda i, b: (i, 0, 0)),
+                pl.BlockSpec((source, width), whole),
+                pl.BlockSpec((source, width), whole),
+            ],
+            out_specs=[
+                pl.BlockSpec((QUERIES, width), rows),
+                pl.BlockSpec((source, width), whole),
+                pl.BlockSpec((source, width), whole),
+            ],
+            scratch_shapes=[
+                pltpu.VMEM((pairs, 128, 2 * QUERIES), jnp.float32),
+                pltpu.VMEM((source, width), jnp.float32),
+                pltpu.VMEM((source, width), jnp.float32),
+            ],
+        ),
+        out_shape=[
+            jax.ShapeDtypeStruct((count, width), jnp.bfloat16),
+            jax.ShapeDtypeStruct((source, width), jnp.bfloat16),
+            jax.ShapeDtypeStruct((source, width), jnp.bfloat16),
+        ],
+        compiler_params=pltpu.CompilerParams(vmem_limit_bytes=40 << 20),
+        cost_estimate=pl.CostEstimate(flops=10 * count * 400 * width, bytes_accessed=16 * count * width, transcendentals=0),
+        name="attend_back",
+    )(bounds, low, high, q, grad, out, sums, k, v)
+
+
+def reach(query_ids, key_ids, causal):
+    count = query_ids.shape[0]
+    low = jnp.sum((key_ids[None, :] < query_ids[:, None]).astype(jnp.int32), axis=1)
+    if causal:
+        high = jnp.arange(count, dtype=jnp.int32) + 1
+    else:
+        high = jnp.sum((key_ids[None, :] <= query_ids[:, None]).astype(jnp.int32), axis=1)
+    first = low[::QUERIES] // 16 * 16
+    steps = (high[QUERIES - 1::QUERIES] - first + KEYS - 1) // KEYS
+    return jnp.stack([first, steps]), low[None], high[None]
 
 
 EPSILON = 1e-05
-MASKED = -1000000000.0
+BF = jnp.bfloat16
+F32 = jnp.float32
+
+
+class Links:
+    def __init__(self, mesh):
+        self.dp = mesh.shape["dp"]
+        self.tensor = mesh.shape["tensor"]
+        self.planes = self.dp // 2
+
+    def enter(self):
+        place = lax.axis_index("dp")
+        self.core = place % 2
+        self.plane = place // 2
+        self.chip = lax.axis_index("tensor")
+
+    def move(self, value, target):
+        pairs = []
+        for place in range(self.dp):
+            for chip in range(self.tensor):
+                to = target(place // 2, place % 2, chip)
+                if to is not None:
+                    pairs.append((place * self.tensor + chip, (to[0] * 2 + to[1]) * self.tensor + to[2]))
+        return lax.ppermute(value, ("dp", "tensor"), pairs)
+
+    def other_core(self, value):
+        return self.move(value, lambda plane, core, chip: (plane, 1 - core, chip))
+
+    def across(self, value, step):
+        return self.move(value, lambda plane, core, chip: (plane, core, chip ^ step))
+
+    def plane_pair(self, value, step):
+        return self.move(value, lambda plane, core, chip: (plane ^ step, core, chip))
+
+    def slot(self, value, which):
+        def target(plane, core, chip):
+            step = 3 if which == 3 else which if plane % 2 == 0 else 3 - which
+            return (plane, core, chip ^ step)
+
+        return self.move(value, target)
+
+    def gather_weight(self, own):
+        first = self.slot(own, 1)
+        diagonal = self.slot(first, 2)
+        second = self.plane_pair(first, 1)
+        return [own, first, second, diagonal]
+
+    def plane_sum(self, parts, first):
+        second = 3 - first
+        near = self.slot(parts[first], first)
+        passed = self.slot(parts[3], first)
+        middle = (parts[second].astype(F32) + passed.astype(F32)).astype(BF)
+        far = self.slot(middle, second)
+        return parts[0].astype(F32) + near.astype(F32) + far.astype(F32)
+
+    def line_sum(self, total):
+        if self.planes % 4:
+            low = total.astype(BF)
+            step = 1
+            while step < self.planes:
+                low = (low.astype(F32) + self.plane_pair(low, step).astype(F32)).astype(BF)
+                step *= 2
+            return low
+        inward = {0: 1, 3: 2}
+        outward = {1: 0, 2: 3}
+        middle = {1: 2, 2: 1}
+
+        def along(table):
+            def target(plane, core, chip):
+                to = table.get(plane % 4)
+                return None if to is None else (plane - plane % 4 + to, core, chip)
+
+            return target
+
+        low = (total + self.move(total.astype(BF), along(inward)).astype(F32)).astype(BF)
+        low = (low.astype(F32) + self.move(low, along(middle)).astype(F32)).astype(BF)
+        step = 4
+        while step < self.planes:
+            low = (low.astype(F32) + self.plane_pair(low, step).astype(F32)).astype(BF)
+            step *= 2
+        back = self.move(low, along(outward))
+        inner = (self.plane % 4 == 1) | (self.plane % 4 == 2)
+        return jnp.where(inner, low, back)
+
+    def weight_total(self, parts, first):
+        return self.line_sum(self.plane_sum(parts, first))
+
+    def halves(self, mine, axis):
+        theirs = self.other_core(mine)
+        return jnp.where(
+            self.core == 0,
+            jnp.concatenate([mine, theirs], axis=axis),
+            jnp.concatenate([theirs, mine], axis=axis),
+        )
+
+    def take_half(self, value, axis, which):
+        size = value.shape[axis] // 2
+        return lax.dynamic_slice_in_dim(value, which * size, size, axis)
+
+    def swap_parts(self, parts):
+        got = [lax.dynamic_index_in_dim(parts, self.chip, 0, keepdims=False)]
+        for step in range(1, self.tensor):
+            got.append(self.across(lax.dynamic_index_in_dim(parts, self.chip ^ step, 0, keepdims=False), step))
+        got = jnp.stack(got)
+        return jnp.stack(
+            [lax.dynamic_index_in_dim(got, self.chip ^ at, 0, keepdims=False) for at in range(self.tensor)]
+        )
+
+    def to_row(self, value):
+        keep = self.take_half(value, 1, self.core)
+        theirs = self.other_core(self.take_half(value, 1, 1 - self.core))
+        rows = jnp.where(self.core == 0, jnp.concatenate([keep, theirs]), jnp.concatenate([theirs, keep]))
+        mine = self.swap_parts(rows)
+        both = self.halves(mine[:, None], 1)
+        return both.reshape(-1, value.shape[-1])
+
+    def half_row(self, row):
+        cut = row.reshape(self.tensor, 2, -1, row.shape[-1])
+        return lax.dynamic_index_in_dim(cut, self.core, 1, keepdims=False)
+
+    def other_half_row(self, row):
+        cut = row.reshape(self.tensor, 2, -1, row.shape[-1])
+        return lax.dynamic_index_in_dim(cut, 1 - self.core, 1, keepdims=False)
+
+    def from_row(self, mine):
+        rows = self.swap_parts(mine)
+        keep = self.take_half(rows, 0, self.core)
+        theirs = self.other_core(self.take_half(rows, 0, 1 - self.core))
+        return jnp.where(
+            self.core == 0,
+            jnp.concatenate([keep, theirs], axis=1),
+            jnp.concatenate([theirs, keep], axis=1),
+        )
+
+    def pair_sum(self, partial):
+        low = lax.optimization_barrier(partial.astype(BF))
+        return low.astype(F32) + self.other_core(low).astype(F32)
+
+    def pair_sum_half(self, partial):
+        low = lax.optimization_barrier(partial.astype(BF))
+        return self.half_row(low).astype(F32) + self.other_core(self.other_half_row(low)).astype(F32)
+
+    def chip_sum(self, value):
+        for step in (1, 2):
+            value = value + self.across(value, step)
+        step = 1
+        while step < self.planes:
+            value = value + self.plane_pair(value, step)
+            step *= 2
+        return value
+
+    def quarter_sum(self, parts):
+        total = parts[0]
+        for which in (1, 2, 3):
+            total = total + self.slot(parts[which], which)
+        step = 1
+        while step < self.planes:
+            total = total + self.plane_pair(total, step)
+            step *= 2
+        return total
+
+
+def norm_stats(values):
+    average = jnp.mean(values, axis=-1, keepdims=True)
+    center = values - average
+    inverse = lax.rsqrt(jnp.mean(center * center, axis=-1, keepdims=True) + EPSILON)
+    return center * inverse, inverse
+
+
+def norm_forward(values, gain, shift):
+    unit, _ = norm_stats(values)
+    return (unit * gain + shift).astype(BF)
+
+
+def norm_backward(grad_in, values, gain):
+    unit, inverse = norm_stats(values)
+    scaled = grad_in * gain
+    first_mean = jnp.mean(scaled, axis=-1, keepdims=True)
+    second_mean = jnp.mean(scaled * unit, axis=-1, keepdims=True)
+    grad_values = inverse * (scaled - first_mean - unit * second_mean)
+    return grad_values, jnp.sum(grad_in * unit, axis=0), jnp.sum(grad_in, axis=0)
+
+
+def cat(parts, axis):
+    return jnp.concatenate(parts, axis=axis)
+
+
+def cut_slots(value, axis):
+    return jnp.split(value, 4, axis=axis)
+
+
+def solution(mesh):
+    if mesh.shape["tensor"] != 4:
+        return general_solution(mesh)
+    links = Links(mesh)
+
+    def local(
+        layer_input, memory, grad_out, target_segments, source_segments,
+        self_gain, self_shift, query_weight, query_bias, key_weight, value_weight, value_bias,
+        attend_weight, attend_bias,
+        cross_gain, cross_shift, cross_query, cross_query_bias, cross_key, cross_value, cross_value_bias,
+        cross_attend, cross_attend_bias,
+        feed_gain, feed_shift, inner_weight, inner_bias, outer_weight, outer_bias,
+    ):
+        links.enter()
+        core, chip = links.core, links.chip
+        columns = lambda w: links.take_half(w, 1, core)
+        rows = lambda w: links.take_half(w, 0, core)
+
+        ids = jnp.stack([target_segments, source_segments], axis=1)
+        their_ids = links.other_core(ids)
+        row_ids = jnp.where(core == 0, cat([ids, their_ids], 0), cat([their_ids, ids], 0))
+        row_ids = lax.dynamic_index_in_dim(row_ids, chip, 0, keepdims=False)
+        target_ids, source_ids = row_ids[0], row_ids[1]
+        reach_self = reach(target_ids, target_ids, True)
+        reach_cross = reach(target_ids, source_ids, False)
+
+        biases = cat([rows(b) for b in (query_bias, value_bias, cross_query_bias, cross_value_bias, inner_bias)], 0)
+        bias_slots = [biases] + [links.slot(biases, which) for which in (1, 2, 3)]
+
+        def bias_of(at, size):
+            return cat([b[at:at + size] for b in bias_slots], 0)
+
+        head = columns(query_weight).shape[1]
+        unit = columns(inner_weight).shape[1]
+        bq, bv, bcq, bcv = (bias_of(i * head, head) for i in range(4))
+        bi = bias_of(4 * head, unit)
+
+        inputs = links.to_row(layer_input).astype(F32)
+        wqkv = links.gather_weight(cat([columns(query_weight), columns(key_weight), columns(value_weight)], 1))
+        wo = links.gather_weight(rows(attend_weight))
+        mem = links.to_row(memory)
+        wckv = links.gather_weight(cat([columns(cross_key), columns(cross_value)], 1))
+        wcq = links.gather_weight(columns(cross_query))
+        wco = links.gather_weight(rows(cross_attend))
+        grad_top_low = links.to_row(grad_out)
+        wi = links.gather_weight(columns(inner_weight))
+        wu = links.gather_weight(rows(outer_weight))
+
+        wq = cat([w[:, :head] for w in wqkv], 1)
+        wk = cat([w[:, head:2 * head] for w in wqkv], 1)
+        wv = cat([w[:, 2 * head:] for w in wqkv], 1)
+        wo = cat(wo, 0)
+        wck = cat([w[:, :head] for w in wckv], 1)
+        wcv = cat([w[:, head:] for w in wckv], 1)
+        wcq = cat(wcq, 1)
+        wco = cat(wco, 0)
+
+        n1 = norm_forward(inputs, self_gain, self_shift)
+        q1 = (dot(n1, wq, NN) + bq).astype(BF)
+        k1 = dot(n1, wk, NN).astype(BF)
+        v1 = (dot(n1, wv, NN) + bv).astype(BF)
+        att1, sums1 = attend(q1, k1, v1, *reach_self)
+        hidden1 = inputs + links.pair_sum(dot(att1, wo, NN)) + attend_bias
+
+        k2 = dot(mem, wck, NN).astype(BF)
+        v2 = (dot(mem, wcv, NN) + bcv).astype(BF)
+        n2 = norm_forward(hidden1, cross_gain, cross_shift)
+        q2 = (dot(n2, wcq, NN) + bcq).astype(BF)
+        att2, sums2 = attend(q2, k2, v2, *reach_cross)
+        hidden2 = hidden1 + links.pair_sum(dot(att2, wco, NN)) + cross_attend_bias
+
+        n3 = norm_forward(hidden2, feed_gain, feed_shift)
+        active, slope = [], []
+        for s in range(4):
+            pre = dot(n3, wi[s], NN) + bi[s * unit:(s + 1) * unit]
+            sigmoid = jax.nn.sigmoid(pre)
+            active.append((pre * sigmoid).astype(BF))
+            slope.append((sigmoid * (1.0 + pre * (1.0 - sigmoid))).astype(BF))
+
+        grad_top = grad_top_low.astype(F32)
+        g_outer = [dot(active[s], grad_top_low, TN).astype(BF) for s in range(4)]
+        grad_inner = [
+            (dot(grad_top_low, wu[s], NT) * slope[s].astype(F32)).astype(BF) for s in range(4)
+        ]
+        g_inner = [dot(n3, grad_inner[s], TN).astype(BF) for s in range(4)]
+        grad_norm3 = sum(dot(grad_inner[s], wi[s], NT) for s in range(4))
+        grad_from3, g_feed_gain, g_feed_shift = norm_backward(links.pair_sum(grad_norm3), hidden2, feed_gain)
+        grad_hidden2 = grad_top + grad_from3
+        g_outer_bias = jnp.sum(grad_top, axis=0)
+        t_outer = links.weight_total(g_outer, 1)
+        t_inner = links.weight_total(g_inner, 2)
+
+        out_part = sum(dot(active[s], wu[s], NN) for s in range(4))
+        out_half = links.half_row(hidden2) + links.pair_sum_half(out_part) + outer_bias
+        block_out = links.from_row(out_half.astype(BF))
+
+        gh2 = grad_hidden2.astype(BF)
+        grad_att2 = dot(gh2, wco, NT).astype(BF)
+        dq2, dk2, dv2 = attend_back(q2, k2, v2, grad_att2, att2, sums2, *reach_cross)
+        t_co = links.weight_total(cut_slots(dot(att2, gh2, TN).astype(BF), 0), 1)
+        t_cq = links.weight_total(cut_slots(dot(n2, dq2, TN).astype(BF), 1), 2)
+        t_ck = links.weight_total(cut_slots(dot(mem, dk2, TN).astype(BF), 1), 1)
+        t_cv = links.weight_total(cut_slots(dot(mem, dv2, TN).astype(BF), 1), 2)
+        grad_norm2 = dot(dq2, wcq, NT)
+        grad_from2, g_cross_gain, g_cross_shift = norm_backward(links.pair_sum(grad_norm2), hidden1, cross_gain)
+        grad_hidden1 = grad_hidden2 + grad_from2
+        g_cross_attend_bias = jnp.sum(grad_hidden2, axis=0)
+        mem_part = dot(dk2, wck, NT) + dot(dv2, wcv, NT)
+        memory_grad = links.from_row(links.pair_sum_half(mem_part).astype(BF)).astype(F32)
+
+        gh1 = grad_hidden1.astype(BF)
+        grad_att1 = dot(gh1, wo, NT).astype(BF)
+        dq1, dk1, dv1 = attend_back(q1, k1, v1, grad_att1, att1, sums1, *reach_self)
+        t_o = links.weight_total(cut_slots(dot(att1, gh1, TN).astype(BF), 0), 1)
+        t_q = links.weight_total(cut_slots(dot(n1, dq1, TN).astype(BF), 1), 2)
+        t_k = links.weight_total(cut_slots(dot(n1, dk1, TN).astype(BF), 1), 1)
+        t_v = links.weight_total(cut_slots(dot(n1, dv1, TN).astype(BF), 1), 2)
+        grad_norm1 = dot(dq1, wq, NT) + dot(dk1, wk, NT) + dot(dv1, wv, NT)
+        grad_from1, g_self_gain, g_self_shift = norm_backward(links.pair_sum(grad_norm1), inputs, self_gain)
+        input_half = links.half_row(grad_hidden1 + grad_from1)
+        input_grad = links.from_row(input_half.astype(BF)).astype(F32)
+        g_attend_bias = jnp.sum(grad_hidden1, axis=0)
+
+        shared = links.chip_sum(
+            jnp.stack([
+                g_self_gain, g_self_shift, g_attend_bias, g_cross_gain, g_cross_shift, g_cross_attend_bias,
+                g_feed_gain, g_feed_shift, g_outer_bias,
+            ])
+        )
+        split = cat(
+            [
+                jnp.sum(g.astype(F32), axis=0).reshape(4, -1)
+                for g in (dq1, dv1, dq2, dv2, cat(grad_inner, 1))
+            ],
+            1,
+        )
+        split = links.quarter_sum(split)
+        split_both = links.other_core(split)
+
+        def split_of(at, size):
+            mine, theirs = split[at:at + size], split_both[at:at + size]
+            return jnp.where(core == 0, cat([mine, theirs], 0), cat([theirs, mine], 0))
+
+        full = lambda total, axis: links.halves(total, axis).astype(F32)
+        return (
+            block_out, input_grad, memory_grad,
+            shared[0], shared[1],
+            full(t_q, 1), split_of(0, head), full(t_k, 1), full(t_v, 1), split_of(head, head),
+            full(t_o, 0), shared[2],
+            shared[3], shared[4],
+            full(t_cq, 1), split_of(2 * head, head), full(t_ck, 1), full(t_cv, 1), split_of(3 * head, head),
+            full(t_co, 0), shared[5],
+            shared[6], shared[7],
+            full(t_inner, 1), split_of(4 * head, unit), full(t_outer, 0), shared[8],
+        )
+
+    row, one, by_column, by_row = P("dp", "tensor", None), P(), P(None, "tensor"), P("tensor", None)
+    part, ids = P("tensor"), P("dp", None)
+    return jax.shard_map(
+        local,
+        mesh=mesh,
+        in_specs=(
+            row, row, row, ids, ids,
+            one, one, by_column, part, by_column, by_column, part, by_row, one,
+            one, one, by_column, part, by_column, by_column, part, by_row, one,
+            one, one, by_column, part, by_row, one,
+        ),
+        out_specs=(
+            row, row, row,
+            one, one, by_column, part, by_column, by_column, part, by_row, one,
+            one, one, by_column, part, by_column, by_column, part, by_row, one,
+            one, one, by_column, part, by_row, one,
+        ),
+        check_vma=False,
+    )
+
+
 BLOCK_ROWS = 512
 
 
-def norm_forward(values, gain, shift):
+def general_norm_forward(values, gain, shift):
     average = jnp.mean(values, axis=-1, keepdims=True)
     center = values - average
     inverse = lax.rsqrt(jnp.mean(center * center, axis=-1, keepdims=True) + EPSILON)
@@ -19,7 +599,7 @@
     return ((normed * gain + shift).astype(jnp.bfloat16), normed, inverse)
 
 
-def norm_backward(grad_in, normed, inverse, gain):
+def general_norm_backward(grad_in, normed, inverse, gain):
     scaled = grad_in * gain
     first_mean = jnp.mean(scaled, axis=-1, keepdims=True)
     second_mean = jnp.mean(scaled * normed, axis=-1, keepdims=True)
@@ -44,7 +624,7 @@
 
 
 def next_rows(values, gain, shift):
-    return gather_rows(norm_forward(values, gain, shift)[0])
+    return gather_rows(general_norm_forward(values, gain, shift)[0])
 
 
 def backward_rows(normed_low):
@@ -199,7 +779,7 @@
     )
 
 
-def local(
+def general_local(
     layer_input,
     memory,
     grad_out,
@@ -259,7 +839,7 @@
         )
     )
     grad_top = grad_out.astype(jnp.float32)
-    normed_low3, unit_third, inverse_third = norm_forward(kept_second, feed_gain, feed_shift)
+    normed_low3, unit_third, inverse_third = general_norm_forward(kept_second, feed_gain, feed_shift)
     rows_back3 = backward_rows(normed_low3)
     pre_back = project(rows_back3, inner_weight) + inner_bias
     sigmoid_back = jax.nn.sigmoid(pre_back)
@@ -274,11 +854,11 @@
     grad_inner_weight = outer_sum(rows_back3, grad_inner)
     grad_inner_bias = bias_sum(grad_inner)
     grad_norm3 = reduce_inputs(project_back(grad_inner, inner_weight))
-    grad_from3, grad_feed_gain, grad_feed_shift = norm_backward(
+    grad_from3, grad_feed_gain, grad_feed_shift = general_norm_backward(
         grad_norm3, unit_third, inverse_third, feed_gain
     )
     grad_hidden2 = grad_top + grad_from3
-    normed_low2, unit_second, inverse_second = norm_forward(kept_first, cross_gain, cross_shift)
+    normed_low2, unit_second, inverse_second = general_norm_forward(kept_first, cross_gain, cross_shift)
     rows_back2 = backward_rows(normed_low2)
     query_back2 = (project(rows_back2, cross_query) + cross_query_bias).astype(jnp.bfloat16)
     keys_back2 = project(kept_memory, cross_key).astype(jnp.bfloat16)
@@ -311,11 +891,11 @@
         tiled=True,
     ).astype(jnp.float32)
     grad_norm2 = reduce_inputs(project_back(grad_query2, cross_query))
-    grad_from2, grad_cross_gain, grad_cross_shift = norm_backward(
+    grad_from2, grad_cross_gain, grad_cross_shift = general_norm_backward(
         grad_norm2, unit_second, inverse_second, cross_gain
     )
     grad_hidden1 = grad_hidden2 + grad_from2
-    normed_low1, unit_first, inverse_first = norm_forward(kept_input, self_gain, self_shift)
+    normed_low1, unit_first, inverse_first = general_norm_forward(kept_input, self_gain, self_shift)
     rows_back1 = backward_rows(normed_low1)
     query_back1 = (project(rows_back1, query_weight) + query_bias).astype(jnp.bfloat16)
     keys_back1 = project(rows_back1, key_weight).astype(jnp.bfloat16)
@@ -344,7 +924,7 @@
         + project_back(grad_keys1, key_weight)
         + project_back(grad_values1, value_weight)
     )
-    grad_from1, grad_self_gain, grad_self_shift = norm_backward(
+    grad_from1, grad_self_gain, grad_self_shift = general_norm_backward(
         grad_norm1, unit_first, inverse_first, self_gain
     )
     input_grad = grad_hidden1 + grad_from1
@@ -436,7 +1016,7 @@
     )
 
 
-def solution(mesh):
+def general_solution(mesh):
     placed = (
         P("dp", "tensor", None),
         P("dp", "tensor", None),
@@ -469,7 +1049,7 @@
         P(),
     )
     return jax.shard_map(
-        local,
+        general_local,
         mesh=mesh,
         in_specs=placed,
         out_specs=(

time: 1740 us -> 820 us (0.47)
  waiting for transfers between devices: 1040 us -> 254 us
  matrix products: 345 us -> 89.1 us
  starting transfers between devices: 1.72 us -> 245 us
  Pallas kernels: 0 us -> 54.8 us
  blocking collectives: 54.4 us -> 0 us
  loops' own time: 43.7 us -> 0 us
  other arithmetic: 144 us -> 108 us
  local copies, waits for them, and re-layouts: 89.4 us -> 58.1 us
    reduce_scatter x7 -> x0, waiting for transfers between devices: 455 us -> none  [the longest x3 245 us: reduce_inputs(): lax.psum_scatter(partial_sum, 'tensor', scatter_dimension=1, tiled=True)]
    all_gather x10 -> x0, waiting for transfers between devices: 441 us -> none  [the longest x6 282 us: gather_rows(): return lax.all_gather(values, 'tensor', axis=1, tiled=True)]
    dot_general x100 -> x48, matrix products: 345 us -> 89.1 us  [dot(): return lax.dot_general(a, b, dims, preferred_element_type=jnp.float32)]
    ppermute x0 -> x139, waiting for transfers between devices: none -> 254 us  [move(): return lax.ppermute(value, ('dp', 'tensor'), pairs)]
    ppermute x0 -> x139, starting transfers between devices: none -> 245 us  [move(): return lax.ppermute(value, ('dp', 'tensor'), pairs)]
    psum x1 -> x0, waiting for transfers between devices: 140 us -> none  [local(): lax.psum(grad_query_weight.astype(jnp.bfloat16), 'dp').astype(jnp.float32)]
    pallas_call x0 -> x4, Pallas kernels: none -> 54.8 us  [the longest x2 28.9 us: attend_back(): pl.pallas_call(attend_back_kernel, grid_spec=pltpu.PrefetchScalarGridSpec...]
    psum x2 -> x0, blocking collectives: 54.4 us -> none  [the longest x1 39.9 us: local(): lax.psum((grad_self_gain, grad_self_shift, grad_attend_bias, grad_cross_g...]
  transfers between devices with their start and end apart: 18 -> 139, of which waited for: 17 -> 41; matrix products, arithmetic and copies ran while one was open for 17% -> 28% of each run, Pallas kernels for 0% -> 7%
where the time goes in v1:
time: 820 us; the launch traced here: 815 us
  waiting for transfers between devices  254 us (31%)
  starting transfers between devices  245 us (30%)
  other arithmetic  108 us (13%)
  matrix products  89.1 us (11%)
  local copies, waits for them, and re-layouts  58.1 us (7%)
  Pallas kernels  54.8 us (7%)
    ppermute x139, waiting for transfers between devices, move(): return lax.ppermute(value, ('dp', 'tensor'), pairs)  254 us
    ppermute x139, starting transfers between devices, move(): return lax.ppermute(value, ('dp', 'tensor'), pairs)  245 us
    dot_general x48, matrix products, dot(): return lax.dot_general(a, b, dims, preferred_element_type=jnp.float32)  89.1 us
    unnamed x346, local copies, waits for them, and re-layouts  40.2 us
    pallas_call x2, Pallas kernels, attend_back(): pl.pallas_call(attend_back_kernel, grid_spec=pltpu.PrefetchScalarGridSpec...  28.9 us
    pallas_call x2, Pallas kernels, attend(): pl.pallas_call(attend_kernel, grid_spec=pltpu.PrefetchScalarGridSpec(num_...  26 us
    convert_element_type x10, other arithmetic, local(): full = lambda total, axis: links.halves(total, axis).astype(F32)  24 us
  transfers between devices with their start and end apart: 139, of which 41 were waited for; matrix products, arithmetic and copies ran while one was open for 28% of the time, Pallas kernels for 7%

profile of v1, /device:TPU:1, one launch (start us, length us, event | category | flops | bytes accessed | tf_op | source)
XLA Modules:
  0.0 814.5 jit_solution(13267110956591602362)
XLA Ops:
  29.5 16.2 %collective-permute-done.3 = bf16[128,1024]{1,0:T(8,128)(2,1)S(1)} collective-permute-done((bf16[128,1024]{1,0:T(8,128)(2,1)S(1)}, bf16[128,1024]{1,0:T(8,128)(2,1)S(1)}, u32[]{:S(2)}, u32[]{:S(2)}) %collective-permute-start.3) | collective-permute-done | bytes 262176 | tf_op jit(solution)/shard_map/ppermute | solution.py:246
  57.0 4.2 collective-permute-start.7
  64.3 10.3 %collective-permute-done.8 = bf16[1024,384]{1,0:T(8,128)(2,1)S(1)} collective-permute-done((bf16[1024,384]{1,0:T(8,128)(2,1)}, bf16[1024,384]{1,0:T(8,128)(2,1)S(1)}, u32[]{:S(2)}, u32[]{:S(2)}) %collective-permute-start.8) | collective-permute-done | bytes 786464 | tf_op jit(solution)/shard_map/ppermute | solution.py:246
  80.6 5.5 collective-permute-start.13
  94.2 12.3 %attend.2 = (bf16[1024,512]{1,0:T(8,128)(2,1)S(1)}, f32[8,4,256]{2,1,0:T(4,128)S(1)}) custom-call(s32[2,8]{1,0:T(2,128)S(1)} %pad_add_fusion.1.bounds, s32[1,1024]{1,0:T(1,128)S(1)} %bitcast.215, s32[1,1024]{1,0:T(1,128)S(1)} %iota_add_fusion.high_ref, bf16[1024,512]{1,0:T(8,128)(2,1)S(1)} %add_convert_fusion.16.q_ref, ...), custom_call_target="tpu_custom_call" | custom-call | flops 838860800 | bytes 4194304 | tf_op jit(solution)/shard_map/attend/pallas_call | solution.py:79
  113.7 3.8 collective-permute-done.27
  133.5 13.6 %attend.3 = (bf16[1024,512]{1,0:T(8,128)(2,1)S(1)}, f32[8,4,256]{2,1,0:T(4,128)S(1)}) custom-call(s32[2,8]{1,0:T(2,128)S(1)} %pad_add_fusion.2.bounds, s32[1,1024]{1,0:T(1,128)S(1)} %bitcast.217, s32[1,1024]{1,0:T(1,128)S(1)} %bitcast.219, bf16[1024,512]{1,0:T(8,128)(2,1)S(1)} %add_convert_fusion.14.q_ref, ...), custom_call_target="tpu_custom_call" | custom-call | flops 838860800 | bytes 4194304 | tf_op jit(solution)/shard_map/attend/pallas_call | solution.py:79
  151.8 5.6 collective-permute-start.45
  164.1 5.7 collective-permute-done.44
  171.1 20.9 %collective-permute-done.32 = bf16[512,1024]{1,0:T(8,128)(2,1)} collective-permute-done((bf16[512,1024]{1,0:T(8,128)(2,1)}, bf16[512,1024]{1,0:T(8,128)(2,1)}, u32[]{:S(2)}, u32[]{:S(2)}) %collective-permute-start.32) | collective-permute-done | bytes 1048608 | tf_op jit(solution)/shard_map/ppermute | solution.py:246
  194.7 19.8 %collective-permute-done.31 = bf16[1024,512]{1,0:T(8,128)(2,1)} collective-permute-done((bf16[1024,512]{1,0:T(8,128)(2,1)}, bf16[1024,512]{1,0:T(8,128)(2,1)}, u32[]{:S(2)}, u32[]{:S(2)}) %collective-permute-start.31) | collective-permute-done | bytes 1048608 | tf_op jit(solution)/shard_map/ppermute | solution.py:246
  218.1 3.8 convert_reduce_fusion.1
  287.2 20.0 %collective-permute-done.126 = bf16[1024,512]{0,1:T(8,128)(2,1)S(1)} collective-permute-done((bf16[1024,512]{0,1:T(8,128)(2,1)S(1)}, bf16[1024,512]{0,1:T(8,128)(2,1)S(1)}, u32[]{:S(2)}, u32[]{:S(2)}) %collective-permute-start.126) | collective-permute-done | bytes 1048608 | tf_op jit(solution)/shard_map/ppermute | solution.py:246
  310.2 25.1 %collective-permute-done.39 = bf16[128,1024]{1,0:T(8,128)(2,1)S(1)} collective-permute-done((bf16[128,1024]{1,0:T(8,128)(2,1)S(1)}, bf16[128,1024]{1,0:T(8,128)(2,1)S(1)}, u32[]{:S(2)}, u32[]{:S(2)}) %collective-permute-start.39) | collective-permute-done | bytes 262176 | tf_op jit(solution)/shard_map/ppermute | solution.py:246
  350.1 9.6 %collective-permute-done.127 = bf16[1024,512]{0,1:T(8,128)(2,1)} collective-permute-done((bf16[1024,512]{0,1:T(8,128)(2,1)}, bf16[1024,512]{0,1:T(8,128)(2,1)}, u32[]{:S(2)}, u32[]{:S(2)}) %collective-permute-start.127) | collective-permute-done | bytes 1048608 | tf_op jit(solution)/shard_map/ppermute | solution.py:246
  363.0 20.3 %collective-permute-start.128 = (bf16[1024,512]{0,1:T(8,128)(2,1)S(1)}, bf16[1024,512]{0,1:T(8,128)(2,1)S(1)}, u32[]{:S(2)}, u32[]{:S(2)}) collective-permute-start(bf16[1024,512]{0,1:T(8,128)(2,1)S(1)} %get-tuple-element.320), channel_id=1, source_target_pairs={{0,8},{1,9},{2,10},{3,11},{4,12},{5,13},{6,14},{7,15},{24,16},{25,... | collective-permute-start | bytes 3145736 | tf_op jit(solution)/shard_map/ppermute | solution.py:246
  397.1 15.1 %attend_back.2 = (bf16[1024,512]{1,0:T(8,128)(2,1)S(1)}, bf16[1024,512]{1,0:T(8,128)(2,1)S(1)}, bf16[1024,512]{1,0:T(8,128)(2,1)S(1)}) custom-call(s32[2,8]{1,0:T(2,128)S(1)} %pad_add_fusion.2.bounds, s32[1,1024]{1,0:T(1,128)S(1)} %bitcast.218, s32[1,1024]{1,0:T(1,128)S(1)} %bitcast.220, bf16[1024,512]{1,0:T(8,128)(2,1)S(1)} %copy-done.11, ...), custom_call_target="tpu_custom_call" | custom-call | flops 2097152000 | bytes 8388608 | tf_op jit(solution)/shard_map/attend_back/pallas_call | solution.py:173
  431.0 7.4 collective-permute-done.112
  443.3 4.0 collective-permute-done.99
  450.3 21.5 %collective-permute-start.135 = (bf16[512,1024]{0,1:T(8,128)(2,1)S(1)}, bf16[512,1024]{0,1:T(8,128)(2,1)S(1)}, u32[]{:S(2)}, u32[]{:S(2)}) collective-permute-start(bf16[512,1024]{0,1:T(8,128)(2,1)S(1)} %get-tuple-element.322), channel_id=1, source_target_pairs={{0,8},{1,9},{2,10},{3,11},{4,12},{5,13},{6,14},{7,15},{24,16},{25,... | collective-permute-start | bytes 3145736 | tf_op jit(solution)/shard_map/ppermute | solution.py:246
  473.4 7.4 collective-permute-start.48
  482.2 10.4 %collective-permute-done.100 = bf16[1024,128]{0,1:T(8,128)(2,1)S(1)} collective-permute-done((bf16[1024,128]{0,1:T(8,128)(2,1)S(1)}, bf16[1024,128]{0,1:T(8,128)(2,1)S(1)}, u32[]{:S(2)}, u32[]{:S(2)}) %collective-permute-start.100) | collective-permute-done | bytes 262176 | tf_op jit(solution)/shard_map/ppermute | solution.py:246
  492.6 4.1 collective-permute-start.114
  498.3 4.1 collective-permute-start.121
  503.9 12.8 %collective-permute-start.54 = (bf16[4,128,1024]{2,1,0:T(8,128)(2,1)S(1)}, bf16[4,128,1024]{2,1,0:T(8,128)(2,1)S(1)}, u32[]{:S(2)}, u32[]{:S(2)}) collective-permute-start(bf16[4,128,1024]{2,1,0:T(8,128)(2,1)S(1)} %dynamic-slice_bitcast_fusion), channel_id=1, source_target_pairs={{0,4},{1,5},{2,6},{3,7},{4,0},{5,1},{6,2},{7,3},{8,12},{9,13},{10,... | collective-permute-start | bytes 3145736 | tf_op jit(solution)/shard_map/ppermute | solution.py:246
  533.6 6.0 collective-permute-done.56
  543.6 7.5 collective-permute-done.102
  552.4 3.7 collective-permute-done.109
  556.1 7.8 collective-permute-start.103
  564.0 4.7 collective-permute-start.110
  598.9 3.8 multiply_reduce_fusion.1
  609.8 13.7 %attend_back.3 = (bf16[1024,512]{1,0:T(8,128)(2,1)S(1)}, bf16[1024,512]{1,0:T(8,128)(2,1)S(1)}, bf16[1024,512]{1,0:T(8,128)(2,1)S(1)}) custom-call(s32[2,8]{1,0:T(2,128)S(1)} %copy-done.17, s32[1,1024]{1,0:T(1,128)S(1)} %bitcast.216, s32[1,1024]{1,0:T(1,128)S(1)} %copy-done.13, bf16[1024,512]{1,0:T(8,128)(2,1)S(1)} %copy-done.3, ...), custom_call_target="tpu_custom_call" | custom-call | flops 2097152000 | bytes 8388608 | tf_op jit(solution)/shard_map/attend_back/pallas_call | solution.py:173
  638.7 4.2 collective-permute-start.73
  657.8 4.6 collective-permute-done.84
  678.0 4.8 collective-permute-start.66
  682.9 4.7 collective-permute-start.49
  690.5 4.5 collective-permute-done.79
  695.0 4.1 collective-permute-start.93
  701.5 4.8 collective-permute-done.93
  714.9 13.9 %collective-permute-done.68 = bf16[1024,128]{0,1:T(8,128)(2,1)S(1)} collective-permute-done((bf16[1024,128]{0,1:T(8,128)(2,1)S(1)}, bf16[1024,128]{0,1:T(8,128)(2,1)S(1)}, u32[]{:S(2)}, u32[]{:S(2)}) %collective-permute-start.68) | collective-permute-done | bytes 262176 | tf_op jit(solution)/shard_map/ppermute | solution.py:246
  730.1 6.6 collective-permute-done.81
  759.7 4.3 multiply_reduce_fusion.2
  764.2 5.0 multiply_add_fusion
  780.8 6.2 collective-permute-done.51
  790.1 5.2 fusion.12
  795.5 4.3 fusion.13
  799.7 5.3 copy.138
  805.1 5.5 copy.139
  (833 shorter events, 390.9 us)
Async XLA Ops:
  19.3 31.0 %collective-permute-start.6 = (bf16[1024,384]{1,0:T(8,128)(2,1)}, bf16[1024,384]{1,0:T(8,128)(2,1)}, u32[]{:S(2)}, u32[]{:S(2)}) collective-permute-start(bf16[1024,384]{1,0:T(8,128)(2,1)} %pad_maximum_fusion.17), channel_id=1, source_target_pairs={{0,1},{1,0},{2,3},{3,2},{4,5},{5,4},{6,7},{7,6},{8,10},{9,11},{10,... | collective-permute-start | bytes 2359304 | tf_op jit(solution)/shard_map/ppermute | solution.py:246
  26.8 23.4 %collective-permute-start.1 = (bf16[128,1024]{1,0:T(8,128)(2,1)S(1)}, bf16[128,1024]{1,0:T(8,128)(2,1)S(1)}, u32[]{:S(2)}, u32[]{:S(2)}) collective-permute-start(bf16[128,1024]{1,0:T(8,128)(2,1)S(1)} %get-tuple-element.267), channel_id=1, source_target_pairs={{0,1},{1,0},{2,3},{3,2},{4,5},{5,4},{6,7},{7,6},{8,9},{9,8},{10,11... | collective-permute-start | bytes 786440 | tf_op jit(solution)/shard_map/ppermute | solution.py:246
  28.2 28.7 %collective-permute-start.22 = (bf16[128,1024]{1,0:T(8,128)(2,1)S(1)}, bf16[128,1024]{1,0:T(8,128)(2,1)S(1)}, u32[]{:S(2)}, u32[]{:S(2)}) collective-permute-start(bf16[128,1024]{1,0:T(8,128)(2,1)S(1)} %get-tuple-element.255), channel_id=1, source_target_pairs={{0,3},{1,2},{2,1},{3,0},{4,7},{5,6},{6,5},{7,4},{8,11},{9,10},{10,... | collective-permute-start | bytes 786440 | tf_op jit(solution)/shard_map/ppermute | solution.py:246
  50.4 24.2 %collective-permute-start.8 = (bf16[1024,384]{1,0:T(8,128)(2,1)}, bf16[1024,384]{1,0:T(8,128)(2,1)S(1)}, u32[]{:S(2)}, u32[]{:S(2)}) collective-permute-start(bf16[1024,384]{1,0:T(8,128)(2,1)} %collective-permute-done.6), channel_id=1, source_target_pairs={{0,2},{1,3},{2,0},{3,1},{4,6},{5,7},{6,4},{7,5},{8,9},{9,8},{10,11... | collective-permute-start | bytes 2359304 | tf_op jit(solution)/shard_map/ppermute | solution.py:246
  52.0 34.1 %collective-permute-start.4 = (bf16[4,1,128,1024]{3,2,0,1:T(8,128)(2,1)S(1)}, bf16[4,1,128,1024]{3,2,0,1:T(8,128)(2,1)S(1)}, u32[]{:S(2)}, u32[]{:S(2)}) collective-permute-start(bf16[4,1,128,1024]{3,2,0,1:T(8,128)(2,1)S(1)} %maximum_bitcast_fusion), channel_id=1, source_target_pairs={{0,4},{1,5},{2,6},{3,7},{4,0},{5,1},{6,2},{7,3},{8,12},{9,13},{10,... | collective-permute-start | bytes 3145736 | tf_op jit(solution)/shard_map/ppermute | solution.py:246
  57.0 22.2 %collective-permute-start.7 = (bf16[1024,384]{1,0:T(8,128)(2,1)}, bf16[1024,384]{1,0:T(8,128)(2,1)S(1)}, u32[]{:S(2)}, u32[]{:S(2)}) collective-permute-start(bf16[1024,384]{1,0:T(8,128)(2,1)} %collective-permute-done.6), channel_id=1, source_target_pairs={{0,8},{1,9},{2,10},{3,11},{4,12},{5,13},{6,14},{7,15},{8,0},{9,1},... | collective-permute-start | bytes 2359304 | tf_op jit(solution)/shard_map/ppermute | solution.py:246
  74.6 34.5 %collective-permute-start.16 = (bf16[1024,128]{1,0:T(8,128)(2,1)S(1)}, bf16[1024,128]{1,0:T(8,128)(2,1)S(1)}, u32[]{:S(2)}, u32[]{:S(2)}) collective-permute-start(bf16[1024,128]{1,0:T(8,128)(2,1)S(1)} %copy-done.82), channel_id=1, source_target_pairs={{0,1},{1,0},{2,3},{3,2},{4,5},{5,4},{6,7},{7,6},{8,10},{9,11},{10,... | collective-permute-start | bytes 786440 | tf_op jit(solution)/shard_map/ppermute | solution.py:246
  76.0 34.3 %collective-permute-start.42 = (bf16[2,128,1024]{2,1,0:T(8,128)(2,1)S(1)}, bf16[2,128,1024]{2,1,0:T(8,128)(2,1)S(1)}, u32[]{:S(2)}, u32[]{:S(2)}) collective-permute-start(bf16[2,128,1024]{2,1,0:T(8,128)(2,1)S(1)} %copy-done.79), channel_id=1, source_target_pairs={{0,4},{1,5},{2,6},{3,7},{4,0},{5,1},{6,2},{7,3},{8,12},{9,13},{10,... | collective-permute-start | bytes 1572872 | tf_op jit(solution)/shard_map/ppermute | solution.py:246
  79.2 27.3 %collective-permute-start.14 = (bf16[128,1024]{1,0:T(8,128)(2,1)S(1)}, bf16[128,1024]{1,0:T(8,128)(2,1)S(1)}, u32[]{:S(2)}, u32[]{:S(2)}) collective-permute-start(bf16[128,1024]{1,0:T(8,128)(2,1)S(1)} %collective-permute-done.12), channel_id=1, source_target_pairs={{0,2},{1,3},{2,0},{3,1},{4,6},{5,7},{6,4},{7,5},{8,9},{9,8},{10,11... | collective-permute-start | bytes 786440 | tf_op jit(solution)/shard_map/ppermute | solution.py:246
  80.6 25.9 %collective-permute-start.13 = (bf16[128,1024]{1,0:T(8,128)(2,1)S(1)}, bf16[128,1024]{1,0:T(8,128)(2,1)S(1)}, u32[]{:S(2)}, u32[]{:S(2)}) collective-permute-start(bf16[128,1024]{1,0:T(8,128)(2,1)S(1)} %collective-permute-done.12), channel_id=1, source_target_pairs={{0,8},{1,9},{2,10},{3,11},{4,12},{5,13},{6,14},{7,15},{8,0},{9,1},... | collective-permute-start | bytes 786440 | tf_op jit(solution)/shard_map/ppermute | solution.py:246
  86.1 25.0 %collective-permute-start.26 = (bf16[1024,256]{1,0:T(8,128)(2,1)S(1)}, bf16[1024,256]{1,0:T(8,128)(2,1)S(1)}, u32[]{:S(2)}, u32[]{:S(2)}) collective-permute-start(bf16[1024,256]{1,0:T(8,128)(2,1)S(1)} %collective-permute-done.24), channel_id=1, source_target_pairs={{0,2},{1,3},{2,0},{3,1},{4,6},{5,7},{6,4},{7,5},{8,9},{9,8},{10,11... | collective-permute-start | bytes 1572872 | tf_op jit(solution)/shard_map/ppermute | solution.py:246
  122.2 24.9 %collective-permute-start.29 = (bf16[128,1024]{1,0:T(8,128)(2,1)S(1)}, bf16[128,1024]{1,0:T(8,128)(2,1)S(1)}, u32[]{:S(2)}, u32[]{:S(2)}) collective-permute-start(bf16[128,1024]{1,0:T(8,128)(2,1)S(1)} %collective-permute-done.27), channel_id=1, source_target_pairs={{0,2},{1,3},{2,0},{3,1},{4,6},{5,7},{6,4},{7,5},{8,9},{9,8},{10,11... | collective-permute-start | bytes 786440 | tf_op jit(solution)/shard_map/ppermute | solution.py:246
  125.0 22.2 %collective-permute-start.28 = (bf16[128,1024]{1,0:T(8,128)(2,1)S(1)}, bf16[128,1024]{1,0:T(8,128)(2,1)S(1)}, u32[]{:S(2)}, u32[]{:S(2)}) collective-permute-start(bf16[128,1024]{1,0:T(8,128)(2,1)S(1)} %collective-permute-done.27), channel_id=1, source_target_pairs={{0,8},{1,9},{2,10},{3,11},{4,12},{5,13},{6,14},{7,15},{8,0},{9,1},... | collective-permute-start | bytes 786440 | tf_op jit(solution)/shard_map/ppermute | solution.py:246
  149.8 72.4 %collective-permute-start.30 = (bf16[1024,1024]{1,0:T(8,128)(2,1)}, bf16[1024,1024]{1,0:T(8,128)(2,1)}, u32[]{:S(2)}, u32[]{:S(2)}) collective-permute-start(bf16[1024,1024]{1,0:T(8,128)(2,1)} %convolution_convert_fusion.1), channel_id=1, source_target_pairs={{0,4},{1,5},{2,6},{3,7},{4,0},{5,1},{6,2},{7,3},{8,12},{9,13},{10,... | collective-permute-start | bytes 6291464 | tf_op jit(solution)/shard_map/ppermute | solution.py:246
  158.8 33.1 %collective-permute-start.32 = (bf16[512,1024]{1,0:T(8,128)(2,1)}, bf16[512,1024]{1,0:T(8,128)(2,1)}, u32[]{:S(2)}, u32[]{:S(2)}) collective-permute-start(bf16[512,1024]{1,0:T(8,128)(2,1)} %constant_dynamic-slice_fusion.27), channel_id=1, source_target_pairs={{0,1},{1,0},{2,3},{3,2},{4,5},{5,4},{6,7},{7,6},{8,10},{9,11},{10,... | collective-permute-start | bytes 3145736 | tf_op jit(solution)/shard_map/ppermute | solution.py:246
  164.1 50.3 %collective-permute-start.31 = (bf16[1024,512]{1,0:T(8,128)(2,1)}, bf16[1024,512]{1,0:T(8,128)(2,1)}, u32[]{:S(2)}, u32[]{:S(2)}) collective-permute-start(bf16[1024,512]{1,0:T(8,128)(2,1)} %constant_dynamic-slice_fusion.28), channel_id=1, source_target_pairs={{0,1},{1,0},{2,3},{3,2},{4,5},{5,4},{6,7},{7,6},{8,10},{9,11},{10,... | collective-permute-start | bytes 3145736 | tf_op jit(solution)/shard_map/ppermute | solution.py:246
  170.2 44.7 %collective-permute-start.46 = (bf16[4,1,128,1024]{3,2,0,1:T(8,128)(2,1)S(1)}, bf16[4,1,128,1024]{3,2,0,1:T(8,128)(2,1)S(1)}, u32[]{:S(2)}, u32[]{:S(2)}) collective-permute-start(bf16[4,1,128,1024]{3,2,0,1:T(8,128)(2,1)S(1)} %maximum_bitcast_fusion.2), channel_id=1, source_target_pairs={{0,4},{1,5},{2,6},{3,7},{4,0},{5,1},{6,2},{7,3},{8,12},{9,13},{10,... | collective-permute-start | bytes 3145736 | tf_op jit(solution)/shard_map/ppermute | solution.py:246
  192.0 58.4 %collective-permute-start.34 = (bf16[512,1024]{1,0:T(8,128)(2,1)}, bf16[512,1024]{1,0:T(8,128)(2,1)S(1)}, u32[]{:S(2)}, u32[]{:S(2)}) collective-permute-start(bf16[512,1024]{1,0:T(8,128)(2,1)} %collective-permute-done.32), channel_id=1, source_target_pairs={{0,8},{1,9},{2,10},{3,11},{4,12},{5,13},{6,14},{7,15},{8,0},{9,1},... | collective-permute-start | bytes 3145736 | tf_op jit(solution)/shard_map/ppermute | solution.py:246
  192.5 62.3 %collective-permute-start.36 = (bf16[512,1024]{1,0:T(8,128)(2,1)}, bf16[512,1024]{1,0:T(8,128)(2,1)S(1)}, u32[]{:S(2)}, u32[]{:S(2)}) collective-permute-start(bf16[512,1024]{1,0:T(8,128)(2,1)} %collective-permute-done.32), channel_id=1, source_target_pairs={{0,2},{1,3},{2,0},{3,1},{4,6},{5,7},{6,4},{7,5},{8,9},{9,8},{10,11... | collective-permute-start | bytes 3145736 | tf_op jit(solution)/shard_map/ppermute | solution.py:246
  214.4 24.1 %collective-permute-start.33 = (bf16[1024,512]{1,0:T(8,128)(2,1)}, bf16[1024,512]{1,0:T(8,128)(2,1)S(1)}, u32[]{:S(2)}, u32[]{:S(2)}) collective-permute-start(bf16[1024,512]{1,0:T(8,128)(2,1)} %collective-permute-done.31), channel_id=1, source_target_pairs={{0,8},{1,9},{2,10},{3,11},{4,12},{5,13},{6,14},{7,15},{8,0},{9,1},... | collective-permute-start | bytes 3145736 | tf_op jit(solution)/shard_map/ppermute | solution.py:246
  215.9 27.4 %collective-permute-start.35 = (bf16[1024,512]{1,0:T(8,128)(2,1)}, bf16[1024,512]{1,0:T(8,128)(2,1)S(1)}, u32[]{:S(2)}, u32[]{:S(2)}) collective-permute-start(bf16[1024,512]{1,0:T(8,128)(2,1)} %collective-permute-done.31), channel_id=1, source_target_pairs={{0,2},{1,3},{2,0},{3,1},{4,6},{5,7},{6,4},{7,5},{8,9},{9,8},{10,11... | collective-permute-start | bytes 3145736 | tf_op jit(solution)/shard_map/ppermute | solution.py:246
  256.7 25.6 %collective-permute-start.37 = (bf16[4,128,1024]{2,1,0:T(8,128)(2,1)S(1)}, bf16[4,128,1024]{2,1,0:T(8,128)(2,1)}, u32[]{:S(2)}, u32[]{:S(2)}) collective-permute-start(bf16[4,128,1024]{2,1,0:T(8,128)(2,1)S(1)} %dynamic-slice_bitcast_fusion.1), channel_id=1, source_target_pairs={{0,4},{1,5},{2,6},{3,7},{4,0},{5,1},{6,2},{7,3},{8,12},{9,13},{10,... | collective-permute-start | bytes 3145736 | tf_op jit(solution)/shard_map/ppermute | solution.py:246
  276.7 30.4 %collective-permute-start.126 = (bf16[1024,512]{0,1:T(8,128)(2,1)S(1)}, bf16[1024,512]{0,1:T(8,128)(2,1)S(1)}, u32[]{:S(2)}, u32[]{:S(2)}) collective-permute-start(bf16[1024,512]{0,1:T(8,128)(2,1)S(1)} %copy-done.138), channel_id=1, source_target_pairs={{0,2},{1,3},{2,0},{3,1},{4,6},{5,7},{6,4},{7,5},{8,9},{9,8},{10,11... | collective-permute-start | bytes 3145736 | tf_op jit(solution)/shard_map/ppermute | solution.py:246
  280.3 106.4 %collective-permute-start.47 = (bf16[1024,1024]{1,0:T(8,128)(2,1)S(1)}, bf16[1024,1024]{1,0:T(8,128)(2,1)}, u32[]{:S(2)}, u32[]{:S(2)}) collective-permute-start(bf16[1024,1024]{1,0:T(8,128)(2,1)S(1)} %add_convert_fusion.2), channel_id=1, source_target_pairs={{0,4},{1,5},{2,6},{3,7},{4,0},{5,1},{6,2},{7,3},{8,12},{9,13},{10,... | collective-permute-start | bytes 6291464 | tf_op jit(solution)/shard_map/ppermute | solution.py:246
  280.6 69.5 %collective-permute-start.125 = (bf16[1024,512]{0,1:T(8,128)(2,1)}, bf16[1024,512]{0,1:T(8,128)(2,1)}, u32[]{:S(2)}, u32[]{:S(2)}) collective-permute-start(bf16[1024,512]{0,1:T(8,128)(2,1)} %convolution_convert_fusion.5), channel_id=1, source_target_pairs={{0,2},{1,3},{2,0},{3,1},{4,6},{5,7},{6,4},{7,5},{8,9},{9,8},{10,11... | collective-permute-start | bytes 3145736 | tf_op jit(solution)/shard_map/ppermute | solution.py:246
  284.3 25.8 %collective-permute-start.40 = (bf16[128,1024]{1,0:T(8,128)(2,1)S(1)}, bf16[128,1024]{1,0:T(8,128)(2,1)S(1)}, u32[]{:S(2)}, u32[]{:S(2)}) collective-permute-start(bf16[128,1024]{1,0:T(8,128)(2,1)S(1)} %get-tuple-element.247), channel_id=1, source_target_pairs={{0,3},{1,2},{2,1},{3,0},{4,7},{5,6},{6,5},{7,4},{8,11},{9,10},{10,... | collective-permute-start | bytes 786440 | tf_op jit(solution)/shard_map/ppermute | solution.py:246
  285.7 49.5 %collective-permute-start.39 = (bf16[128,1024]{1,0:T(8,128)(2,1)S(1)}, bf16[128,1024]{1,0:T(8,128)(2,1)S(1)}, u32[]{:S(2)}, u32[]{:S(2)}) collective-permute-start(bf16[128,1024]{1,0:T(8,128)(2,1)S(1)} %get-tuple-element.248), channel_id=1, source_target_pairs={{0,2},{1,3},{2,0},{3,1},{4,6},{5,7},{6,4},{7,5},{8,10},{9,11},{10,... | collective-permute-start | bytes 786440 | tf_op jit(solution)/shard_map/ppermute | solution.py:246
  307.2 29.7 %collective-permute-start.38 = (bf16[128,1024]{1,0:T(8,128)(2,1)S(1)}, bf16[128,1024]{1,0:T(8,128)(2,1)S(1)}, u32[]{:S(2)}, u32[]{:S(2)}) collective-permute-start(bf16[128,1024]{1,0:T(8,128)(2,1)S(1)} %get-tuple-element.249), channel_id=1, source_target_pairs={{0,1},{1,0},{2,3},{3,2},{4,5},{5,4},{6,7},{7,6},{8,9},{9,8},{10,11... | collective-permute-start | bytes 786440 | tf_op jit(solution)/shard_map/ppermute | solution.py:246
  310.2 31.9 %collective-permute-start.133 = (bf16[512,1024]{0,1:T(8,128)(2,1)S(1)}, bf16[512,1024]{0,1:T(8,128)(2,1)S(1)}, u32[]{:S(2)}, u32[]{:S(2)}) collective-permute-start(bf16[512,1024]{0,1:T(8,128)(2,1)S(1)} %copy-done.135), channel_id=1, source_target_pairs={{0,1},{1,0},{2,3},{3,2},{4,5},{5,4},{6,7},{7,6},{8,10},{9,11},{10,... | collective-permute-start | bytes 3145736 | tf_op jit(solution)/shard_map/ppermute | solution.py:246
  335.3 24.5 %collective-permute-start.127 = (bf16[1024,512]{0,1:T(8,128)(2,1)}, bf16[1024,512]{0,1:T(8,128)(2,1)}, u32[]{:S(2)}, u32[]{:S(2)}) collective-permute-start(bf16[1024,512]{0,1:T(8,128)(2,1)} %add_convert_fusion.12), channel_id=1, source_target_pairs={{0,1},{1,0},{2,3},{3,2},{4,5},{5,4},{6,7},{7,6},{8,10},{9,11},{10,... | collective-permute-start | bytes 3145736 | tf_op jit(solution)/shard_map/ppermute | solution.py:246
  342.1 41.2 %collective-permute-start.132 = (bf16[512,1024]{0,1:T(8,128)(2,1)}, bf16[512,1024]{0,1:T(8,128)(2,1)}, u32[]{:S(2)}, u32[]{:S(2)}) collective-permute-start(bf16[512,1024]{0,1:T(8,128)(2,1)} %convolution_convert_fusion.9), channel_id=1, source_target_pairs={{0,1},{1,0},{2,3},{3,2},{4,5},{5,4},{6,7},{7,6},{8,10},{9,11},{10,... | collective-permute-start | bytes 3145736 | tf_op jit(solution)/shard_map/ppermute | solution.py:246
  343.4 40.0 %collective-permute-start.134 = (bf16[512,1024]{0,1:T(8,128)(2,1)}, bf16[512,1024]{0,1:T(8,128)(2,1)}, u32[]{:S(2)}, u32[]{:S(2)}) collective-permute-start(bf16[512,1024]{0,1:T(8,128)(2,1)} %add_convert_fusion.9), channel_id=1, source_target_pairs={{0,2},{1,3},{2,0},{3,1},{4,6},{5,7},{6,4},{7,5},{8,9},{9,8},{10,11... | collective-permute-start | bytes 3145736 | tf_op jit(solution)/shard_map/ppermute | solution.py:246
  363.0 154.7 %collective-permute-start.128 = (bf16[1024,512]{0,1:T(8,128)(2,1)S(1)}, bf16[1024,512]{0,1:T(8,128)(2,1)S(1)}, u32[]{:S(2)}, u32[]{:S(2)}) collective-permute-start(bf16[1024,512]{0,1:T(8,128)(2,1)S(1)} %get-tuple-element.320), channel_id=1, source_target_pairs={{0,8},{1,9},{2,10},{3,11},{4,12},{5,13},{6,14},{7,15},{24,16},{25,... | collective-permute-start | bytes 3145736 | tf_op jit(solution)/shard_map/ppermute | solution.py:246
  447.3 24.5 %collective-permute-start.113 = (bf16[1024,128]{0,1:T(8,128)(2,1)S(1)}, bf16[1024,128]{0,1:T(8,128)(2,1)S(1)}, u32[]{:S(2)}, u32[]{:S(2)}) collective-permute-start(bf16[1024,128]{0,1:T(8,128)(2,1)S(1)} %add_convert_fusion.22), channel_id=1, source_target_pairs={{0,1},{1,0},{2,3},{3,2},{4,5},{5,4},{6,7},{7,6},{8,10},{9,11},{10,... | collective-permute-start | bytes 786440 | tf_op jit(solution)/shard_map/ppermute | solution.py:246
  447.5 25.9 %collective-permute-start.118 = (bf16[128,1024]{1,0:T(8,128)(2,1)S(1)}, bf16[128,1024]{1,0:T(8,128)(2,1)S(1)}, u32[]{:S(2)}, u32[]{:S(2)}) collective-permute-start(bf16[128,1024]{1,0:T(8,128)(2,1)S(1)} %get-tuple-element.194), channel_id=1, source_target_pairs={{0,1},{1,0},{2,3},{3,2},{4,5},{5,4},{6,7},{7,6},{8,10},{9,11},{10,... | collective-permute-start | bytes 786440 | tf_op jit(solution)/shard_map/ppermute | solution.py:246
  449.0 31.8 %collective-permute-start.120 = (bf16[128,1024]{1,0:T(8,128)(2,1)S(1)}, bf16[128,1024]{1,0:T(8,128)(2,1)S(1)}, u32[]{:S(2)}, u32[]{:S(2)}) collective-permute-start(bf16[128,1024]{1,0:T(8,128)(2,1)S(1)} %add_convert_fusion.19), channel_id=1, source_target_pairs={{0,2},{1,3},{2,0},{3,1},{4,6},{5,7},{6,4},{7,5},{8,9},{9,8},{10,11... | collective-permute-start | bytes 786440 | tf_op jit(solution)/shard_map/ppermute | solution.py:246
  450.3 70.7 %collective-permute-start.135 = (bf16[512,1024]{0,1:T(8,128)(2,1)S(1)}, bf16[512,1024]{0,1:T(8,128)(2,1)S(1)}, u32[]{:S(2)}, u32[]{:S(2)}) collective-permute-start(bf16[512,1024]{0,1:T(8,128)(2,1)S(1)} %get-tuple-element.322), channel_id=1, source_target_pairs={{0,8},{1,9},{2,10},{3,11},{4,12},{5,13},{6,14},{7,15},{24,16},{25,... | collective-permute-start | bytes 3145736 | tf_op jit(solution)/shard_map/ppermute | solution.py:246
  473.4 125.5 %collective-permute-start.48 = (bf16[1024,1024]{1,0:T(8,128)(2,1)}, bf16[1024,1024]{1,0:T(8,128)(2,1)S(1)}, u32[]{:S(2)}, u32[]{:S(2)}) collective-permute-start(bf16[1024,1024]{1,0:T(8,128)(2,1)} %convolution_convert_fusion), channel_id=1, source_target_pairs={{0,4},{1,5},{2,6},{3,7},{4,0},{5,1},{6,2},{7,3},{8,12},{9,13},{10,... | collective-permute-start | bytes 6291464 | tf_op jit(solution)/shard_map/ppermute | solution.py:246
  529.1 64.6 %collective-permute-start.129 = (bf16[1024,512]{0,1:T(8,128)(2,1)S(1)}, bf16[1024,512]{0,1:T(8,128)(2,1)}, u32[]{:S(2)}, u32[]{:S(2)}) collective-permute-start(bf16[1024,512]{0,1:T(8,128)(2,1)S(1)} %add_convert_fusion.11), channel_id=1, source_target_pairs={{8,16},{9,17},{10,18},{11,19},{12,20},{13,21},{14,22},{15,23},{16,... | collective-permute-start | bytes 3145736 | tf_op jit(solution)/shard_map/ppermute | solution.py:246
  540.9 23.0 %collective-permute-start.116 = (bf16[1024,128]{0,1:T(8,128)(2,1)S(1)}, bf16[1024,128]{0,1:T(8,128)(2,1)S(1)}, u32[]{:S(2)}, u32[]{:S(2)}) collective-permute-start(bf16[1024,128]{0,1:T(8,128)(2,1)S(1)} %add_convert_fusion.20), channel_id=1, source_target_pairs={{8,0},{9,1},{10,2},{11,3},{12,4},{13,5},{14,6},{15,7},{16,24},{17,... | collective-permute-start | bytes 786440 | tf_op jit(solution)/shard_map/ppermute | solution.py:246
  569.4 27.6 %collective-permute-start.136 = (bf16[512,1024]{0,1:T(8,128)(2,1)}, bf16[512,1024]{0,1:T(8,128)(2,1)}, u32[]{:S(2)}, u32[]{:S(2)}) collective-permute-start(bf16[512,1024]{0,1:T(8,128)(2,1)} %add_convert_fusion.8), channel_id=1, source_target_pairs={{8,16},{9,17},{10,18},{11,19},{12,20},{13,21},{14,22},{15,23},{16,... | collective-permute-start | bytes 3145736 | tf_op jit(solution)/shard_map/ppermute | solution.py:246
  595.6 111.6 %collective-permute-start.130 = (bf16[1024,512]{0,1:T(8,128)(2,1)S(1)}, bf16[1024,512]{0,1:T(8,128)(2,1)S(1)}, u32[]{:S(2)}, u32[]{:S(2)}) collective-permute-start(bf16[1024,512]{0,1:T(8,128)(2,1)S(1)} %add_convert_fusion.10), channel_id=1, source_target_pairs={{8,0},{9,1},{10,2},{11,3},{12,4},{13,5},{14,6},{15,7},{16,24},{17,... | collective-permute-start | bytes 3145736 | tf_op jit(solution)/shard_map/ppermute | solution.py:246
  638.3 28.1 %collective-permute-start.63 = (bf16[1024,128]{0,1:T(8,128)(2,1)S(1)}, bf16[1024,128]{0,1:T(8,128)(2,1)S(1)}, u32[]{:S(2)}, u32[]{:S(2)}) collective-permute-start(bf16[1024,128]{0,1:T(8,128)(2,1)S(1)} %get-tuple-element.208), channel_id=1, source_target_pairs={{0,2},{1,3},{2,0},{3,1},{4,6},{5,7},{6,4},{7,5},{8,9},{9,8},{10,11... | collective-permute-start | bytes 786440 | tf_op jit(solution)/shard_map/ppermute | solution.py:246
  676.7 32.2 %collective-permute-start.137 = (bf16[512,1024]{0,1:T(8,128)(2,1)S(1)}, bf16[512,1024]{0,1:T(8,128)(2,1)S(1)}, u32[]{:S(2)}, u32[]{:S(2)}) collective-permute-start(bf16[512,1024]{0,1:T(8,128)(2,1)S(1)} %add_convert_fusion.7), channel_id=1, source_target_pairs={{8,0},{9,1},{10,2},{11,3},{12,4},{13,5},{14,6},{15,7},{16,24},{17,... | collective-permute-start | bytes 3145736 | tf_op jit(solution)/shard_map/ppermute | solution.py:246
  682.9 76.7 %collective-permute-start.49 = (bf16[1024,1024]{1,0:T(8,128)(2,1)S(1)}, bf16[1024,1024]{1,0:T(8,128)(2,1)}, u32[]{:S(2)}, u32[]{:S(2)}) collective-permute-start(bf16[1024,1024]{1,0:T(8,128)(2,1)S(1)} %add_convert_fusion.1), channel_id=1, source_target_pairs={{0,4},{1,5},{2,6},{3,7},{4,0},{5,1},{6,2},{7,3},{8,12},{9,13},{10,... | collective-permute-start | bytes 6291464 | tf_op jit(solution)/shard_map/ppermute | solution.py:246
  710.0 80.2 %collective-permute-start.131 = (bf16[1024,512]{0,1:T(8,128)(2,1)}, bf16[1024,512]{0,1:T(8,128)(2,1)}, u32[]{:S(2)}, u32[]{:S(2)}) collective-permute-start(bf16[1024,512]{0,1:T(8,128)(2,1)} %broadcast_select_fusion.1), channel_id=1, source_target_pairs={{0,4},{1,5},{2,6},{3,7},{4,0},{5,1},{6,2},{7,3},{8,12},{9,13},{10,... | collective-permute-start | bytes 3145736 | tf_op jit(solution)/shard_map/ppermute | solution.py:246
  711.9 83.5 %collective-permute-start.138 = (bf16[512,1024]{0,1:T(8,128)(2,1)S(1)}, bf16[512,1024]{0,1:T(8,128)(2,1)}, u32[]{:S(2)}, u32[]{:S(2)}) collective-permute-start(bf16[512,1024]{0,1:T(8,128)(2,1)S(1)} %broadcast_select_fusion), channel_id=1, source_target_pairs={{0,4},{1,5},{2,6},{3,7},{4,0},{5,1},{6,2},{7,3},{8,12},{9,13},{10,... | collective-permute-start | bytes 3145736 | tf_op jit(solution)/shard_map/ppermute | solution.py:246
  713.5 23.2 %collective-permute-start.81 = (bf16[1024,128]{0,1:T(8,128)(2,1)S(1)}, bf16[1024,128]{0,1:T(8,128)(2,1)S(1)}, u32[]{:S(2)}, u32[]{:S(2)}) collective-permute-start(bf16[1024,128]{0,1:T(8,128)(2,1)S(1)} %add_convert_fusion.35), channel_id=1, source_target_pairs={{8,0},{9,1},{10,2},{11,3},{12,4},{13,5},{14,6},{15,7},{16,24},{17,... | collective-permute-start | bytes 786440 | tf_op jit(solution)/shard_map/ppermute | solution.py:246
  (256 other events, 2904.4 us)

commit v2 on v0

--- a/solution.py
+++ b/solution.py
@@ -1,17 +1,1282 @@
 import jax
 import jax.numpy as jnp
 from jax import lax
+from jax.experimental import pallas as pl
+from jax.experimental.pallas import tpu as pltpu
 from jax.sharding import PartitionSpec as P
 
 HD = 64
+MASKED = -1000000000.0
+QUERIES = 128
+KEYS = 256
+NT = (((1,), (1,)), ((), ()))
+TN = (((0,), (0,)), ((), ()))
+NN = (((1,), (0,)), ((), ()))
+
+
+def dot(a, b, dims):
+    return lax.dot_general(a, b, dims, preferred_element_type=jnp.float32)
+
+
+def both_heads(block):
+    first = lax.broadcasted_iota(jnp.int32, block.shape, 1) < HD
+    zero = jnp.zeros_like(block)
+    return jnp.concatenate([jnp.where(first, block, zero), jnp.where(first, zero, block)], axis=0)
+
+
+def allowed_keys(least, limit, at):
+    key_place = at + lax.broadcasted_iota(jnp.int32, (KEYS, 1), 0)
+    seen = (key_place >= least) & (key_place < limit)
+    return jnp.concatenate([seen, seen], axis=1)
+
+
+def attend_step(queries, k_ref, k_at, v_at, rows, seen, acc, top, total):
+    pairs = range(len(queries))
+    keys = [k_ref[rows, k_at + p * 128:k_at + p * 128 + 128] for p in pairs]
+    values = [k_ref[rows, v_at + p * 128:v_at + p * 128 + 128] for p in pairs]
+    scores = [jnp.where(seen, dot(keys[p], queries[p], NT), MASKED) for p in pairs]
+    before = [top[p:p + 1] for p in pairs]
+    now = [jnp.maximum(before[p], jnp.max(scores[p], axis=0, keepdims=True)) for p in pairs]
+    weight = [jnp.exp(scores[p] - now[p]) for p in pairs]
+    keep = [jnp.exp(before[p] - now[p]) for p in pairs]
+    added = [dot(values[p], weight[p].astype(jnp.bfloat16), TN) for p in pairs]
+    sums = [jnp.sum(weight[p], axis=0, keepdims=True) for p in pairs]
+    for p in pairs:
+        top[p:p + 1] = now[p]
+        total[p:p + 1] = total[p:p + 1] * keep[p] + sums[p]
+        acc[p] = acc[p] * keep[p] + added[p]
+
+
+def attend_back_step(queries, grads, fixes, sums, k_ref, k_at, v_at, rows, seen, acc, acc_k, acc_v):
+    pairs = range(len(queries))
+    cuts = [slice(p * 128, (p + 1) * 128) for p in pairs]
+    keys = [k_ref[rows, k_at + p * 128:k_at + p * 128 + 128] for p in pairs]
+    values = [k_ref[rows, v_at + p * 128:v_at + p * 128 + 128] for p in pairs]
+    scores = [dot(keys[p], queries[p], NT) for p in pairs]
+    dprob = [dot(values[p], grads[p], NT) for p in pairs]
+    prob = [jnp.exp(jnp.where(seen, scores[p] - sums[p], MASKED)) for p in pairs]
+    low = [prob[p].astype(jnp.bfloat16) for p in pairs]
+    dscore = [(prob[p] * (dprob[p] - fixes[p])).astype(jnp.bfloat16) for p in pairs]
+    added_v = [dot(low[p], grads[p], NN) for p in pairs]
+    added_k = [dot(dscore[p], queries[p], NN) for p in pairs]
+    added_q = [dot(keys[p], dscore[p], TN) for p in pairs]
+    for p in pairs:
+        acc_v[rows, cuts[p]] += added_v[p]
+        acc_k[rows, cuts[p]] += added_k[p]
+        acc[p] += added_q[p]
 
 
 EPSILON = 1e-05
-MASKED = -1000000000.0
+BF = jnp.bfloat16
+F32 = jnp.float32
+
+
+def norm_stats(values):
+    average = jnp.mean(values, axis=-1, keepdims=True)
+    center = values - average
+    inverse = lax.rsqrt(jnp.mean(center * center, axis=-1, keepdims=True) + EPSILON)
+    return center * inverse, inverse
+
+
+def norm_forward(values, gain, shift):
+    unit, _ = norm_stats(values)
+    return (unit * gain + shift).astype(BF)
+
+
+class Net:
+    def __init__(self, sems, local_sems):
+        place = lax.axis_index("dp")
+        chip = lax.axis_index("tensor")
+        core, plane = place % 2, place // 2
+        odd = plane % 2
+        beside, over, corner = chip + 1 - 2 * (chip % 2), (chip + 2) % 4, 3 - chip
+        self.chip, self.core_index, self.odd, self.plane = chip, core, odd, plane
+        self.chips = (beside, over, corner)
+        self.core = (plane * 2 + 1 - core, chip)
+        self.first = (place, beside + odd * (over - beside))
+        self.second = (place, over + odd * (beside - over))
+        self.corner = (place, corner)
+        self.near_plane = ((plane + 1 - 2 * odd) * 2 + core, chip)
+        self.far_plane = ((plane + 2) % 4 * 2 + core, chip)
+        self.sems, self.local_sems = sems, local_sems
+        self.count = self.local_count = 0
+        self.unsent, self.unmoved = [], []
+
+    def meet(self):
+        barrier = pltpu.get_barrier_semaphore()
+        partners = (self.core, self.first, self.second, self.corner, self.near_plane, self.far_plane)
+        for partner in partners:
+            pl.semaphore_signal(barrier, inc=1, device_id=partner, device_id_type=pl.DeviceIdType.MESH)
+        pl.semaphore_wait(barrier, len(partners))
+
+    def send(self, source, target, device):
+        copy = pltpu.make_async_remote_copy(
+            src_ref=source,
+            dst_ref=target,
+            send_sem=self.sems.at[0, self.count],
+            recv_sem=self.sems.at[1, self.count],
+            device_id=device,
+            device_id_type=pl.DeviceIdType.MESH,
+        )
+        self.count += 1
+        copy.start()
+        self.unsent.append(copy)
+        return copy
+
+    def move(self, source, target):
+        copy = pltpu.make_async_copy(source, target, self.local_sems.at[self.local_count])
+        self.local_count += 1
+        copy.start()
+        self.unmoved.append(copy)
+        return copy
+
+    def moved(self, copy):
+        copy.wait()
+        self.unmoved = [other for other in self.unmoved if other is not copy]
+
+    def sent(self, copy):
+        copy.wait_send()
+        self.unsent = [other for other in self.unsent if other is not copy]
+
+    def finish(self):
+        for copy in self.unmoved:
+            copy.wait()
+        for copy in self.unsent:
+            copy.wait_send()
+        self.unsent, self.unmoved = [], []
+
+
+def row_in(net, given, rows, row):
+    core, chip = net.core_index, net.chip
+    mine = pl.ds(2 * core, 2)
+    swap = net.send(given.at[:, 1 - core], rows.at[mine], net.core)
+    keep = net.move(given.at[:, core], rows.at[mine])
+    yield
+    net.moved(keep)
+    swap.wait_recv()
+    own = net.move(rows.at[chip], row.at[chip, core])
+    sends = [
+        net.send(rows.at[other], row.at[chip, core], (lax.axis_index("dp"), other)) for other in net.chips
+    ]
+    yield
+    net.moved(own)
+    shares = [net.send(row.at[chip, core], row.at[chip, core], net.core)]
+    for other, copy in zip(net.chips, sends):
+        copy.wait_recv()
+        shares.append(net.send(row.at[other, core], row.at[other, core], net.core))
+    yield
+    for copy in shares:
+        copy.wait_recv()
+
+
+def row_out(net, pieces, rows, result):
+    core, chip = net.core_index, net.chip
+    own = net.move(pieces.at[chip], rows.at[chip])
+    sends = [net.send(pieces.at[other], rows.at[chip], (lax.axis_index("dp"), other)) for other in net.chips]
+    yield
+    net.moved(own)
+    for copy in sends:
+        copy.wait_recv()
+    keep = net.move(rows.at[pl.ds(2 * core, 2)], result.at[:, core])
+    swap = net.send(rows.at[pl.ds(2 * (1 - core), 2)], result.at[:, core], net.core)
+    yield
+    swap.wait_recv()
+    net.moved(keep)
+
+
+class Gather:
+    def __init__(self, net, own, slot, flip=False):
+        self.net, self.slot = net, slot
+        self.one, self.two = (2, 1) if flip else (1, 2)
+        to_one, self.to_two = (net.second, net.first) if flip else (net.first, net.second)
+        self.near = net.send(own, slot(self.one), to_one)
+        self.own = net.move(own, slot(0))
+
+    def relay(self):
+        self.near.wait_recv()
+        self.corner = self.net.send(self.slot(self.one), self.slot(3), self.to_two)
+        self.other = self.net.send(self.slot(self.one), self.slot(self.two), self.net.near_plane)
+
+    def finish(self):
+        self.net.moved(self.own)
+        self.corner.wait_recv()
+        self.other.wait_recv()
+
+
+ANY = pl.BlockSpec(memory_space=pl.ANY)
+VM = pl.BlockSpec(memory_space=pltpu.VMEM)
+SENDS = 160
+
+
+def half_columns(net, weight, width):
+    return weight.at[:, pl.ds(pl.multiple_of(net.core_index * width, width), width)]
+
+
+def half_rows(net, weight, height):
+    return weight.at[pl.ds(pl.multiple_of(net.core_index * height, height), height)]
+
+
+def tile_rows(i, size=256):
+    return pl.ds(pl.multiple_of(i * size, size), size)
+
+
+def call_remote(kernel, ident, ins, in_specs, outs, out_specs, scratch, vmem=48, name=None):
+    return pl.pallas_call(
+        kernel,
+        in_specs=in_specs,
+        out_specs=out_specs,
+        out_shape=outs,
+        scratch_shapes=list(scratch) + [pltpu.SemaphoreType.DMA((2, SENDS)), pltpu.SemaphoreType.DMA((SENDS,))],
+        compiler_params=pltpu.CompilerParams(
+            collective_id=ident, has_side_effects=True, vmem_limit_bytes=vmem << 20
+        ),
+        name=name,
+    )(*ins)
+
+
+def add_up(target, sources, step=64):
+    def some(i, _):
+        cut = pl.ds(pl.multiple_of(i * step, step), step)
+        total = sources[0][cut].astype(F32)
+        for source in sources[1:]:
+            total = total + source[cut].astype(F32)
+        target[cut] = total.astype(BF)
+        return 0
+
+    lax.fori_loop(0, target.shape[0] // step, some, 0)
+
+
+class Line:
+    def __init__(self, net, total, landing, result):
+        self.net, self.total, self.result = net, total, result
+        self.one_in, self.two_in = landing
+        self.size = self.one_in.shape[0]
+
+    def half(self, which):
+        return self.total.at[pl.ds(pl.multiple_of(which * self.size, self.size), self.size)]
+
+    def line0(self):
+        self.line = self.net.send(self.half(1 - self.net.odd), self.one_in, self.net.near_plane)
+
+    def line1(self):
+        self.line.wait_recv()
+        mine = self.half(self.net.odd)
+        add_up(mine, [mine, self.one_in])
+        self.line = self.net.send(mine, self.two_in, self.net.far_plane)
+
+    def line2(self):
+        self.line.wait_recv()
+        place = self.result(self.net.core_index, self.net.odd)
+        add_up(self.two_in, [self.half(self.net.odd), self.two_in])
+        self.net.move(self.two_in, place)
+        self.line = self.net.send(self.two_in, place, self.net.near_plane)
+        self.cores = [self.net.send(self.two_in, place, self.net.core)]
+
+    def line3(self):
+        self.line.wait_recv()
+        place = self.result(self.net.core_index, 1 - self.net.odd)
+        self.cores.append(self.net.send(place, place, self.net.core))
+
+    def end(self):
+        for copy in self.cores:
+            copy.wait_recv()
+
+
+class Scatter:
+    def __init__(self, net, part, first, landing):
+        self.net, self.part = net, part
+        self.near_in, self.pass_in, self.far_in = landing
+        self.one, self.two = (1, 2) if first == 1 else (2, 1)
+        self.to_one, self.to_two = (net.first, net.second) if first == 1 else (net.second, net.first)
+
+    def start(self):
+        self.passed = self.net.send(self.part(3), self.pass_in, self.to_one)
+        self.near = self.net.send(self.part(self.one), self.near_in, self.to_one)
+
+    def middle(self):
+        self.passed.wait_recv()
+        add_up(self.part(self.two), [self.part(self.two), self.pass_in])
+        self.far = self.net.send(self.part(self.two), self.far_in, self.to_two)
+
+    def own(self):
+        self.near.wait_recv()
+        self.far.wait_recv()
+        add_up(self.part(0), [self.part(0), self.near_in, self.far_in])
+
+
+def landing(rows, columns):
+    return [pltpu.VMEM((rows, columns), BF)] * 3
+
+
+def line_landing(rows, columns):
+    return [pltpu.VMEM((rows // 2, columns), BF)] * 2
+
+
+def weight_grad(lhs, rhs, target, start, count, columns=slice(None), size=256):
+    def some(i, _):
+        cut = pl.ds(pl.multiple_of(start + i * size, size), size)
+        target[cut, columns] = dot(lhs(cut), rhs(), TN).astype(BF)
+        return 0
+
+    lax.fori_loop(0, count // size, some, 0)
+
+
+def norm_back_tile(grad_in, values, gain):
+    unit, inverse = norm_stats(values)
+    scaled = grad_in * gain
+    first_mean = jnp.mean(scaled, axis=-1, keepdims=True)
+    second_mean = jnp.mean(scaled * unit, axis=-1, keepdims=True)
+    grad_values = inverse * (scaled - first_mean - unit * second_mean)
+    return grad_values, jnp.sum(grad_in * unit, axis=0, keepdims=True), jnp.sum(grad_in, axis=0, keepdims=True)
+
+
+def head_scatters(net, g_heads, g_out, lands):
+    found = []
+    for kind in range(3):
+        found.append(
+            Scatter(
+                net, lambda s, kind=kind: g_heads.at[:, kind * 512 + s * 128:kind * 512 + s * 128 + 128],
+                (1, 1, 2)[kind], lands[kind * 3:kind * 3 + 3],
+            )
+        )
+    found.append(Scatter(net, lambda s: g_out.at[pl.ds(s * 128, 128)], 2, lands[9:12]))
+    return found
+
+
+def head_lines(net, totals, total_out, full_heads, full_out, lands):
+    lines = []
+    for kind in range(3):
+        lines.append(
+            Line(
+                net, totals(kind), lands[kind * 2:kind * 2 + 2],
+                lambda c, h, kind=kind: full_heads.at[
+                    kind, pl.ds(pl.multiple_of(h * 512, 512), 512), pl.ds(pl.multiple_of(c * 128, 128), 128)
+                ],
+            )
+        )
+    lines.append(
+        Line(
+            net, total_out, lands[6:8],
+            lambda c, h: full_out.at[pl.ds(pl.multiple_of(c * 128 + h * 64, 64), 64)],
+        )
+    )
+    return lines
+
+
+def head_landing(width):
+    return landing(1024, 128) * 3 + landing(128, width)
+
+
+def head_line_landing(width):
+    return line_landing(1024, 128) * 3 + line_landing(128, width)
+
+
+def attend_block(i, q_ref, q_at, k_ref, k_at, v_at, low, high, causal, out_ref, sums_ref, acc, top, total):
+    pairs = range(4)
+    rows = tile_rows(i, QUERIES)
+    queries = [
+        both_heads(q_ref[rows, q_at + p * 128:q_at + p * 128 + 128] * jnp.bfloat16(HD ** -0.5)) for p in pairs
+    ]
+    least, limit = low[pl.ds(i, 1)], high[pl.ds(i, 1)]
+    acc[...] = jnp.zeros_like(acc)
+    total[...] = jnp.zeros_like(total)
+    top[...] = jnp.full_like(top, -1e30)
+
+    def step(j, _):
+        at = pl.multiple_of(j * KEYS, KEYS)
+        seen = allowed_keys(least, limit, at)
+        attend_step(queries, k_ref, k_at, v_at, pl.ds(at, KEYS), seen, acc, top, total)
+        return 0
+
+    lax.fori_loop(0, i // 2 + 1 if causal else k_ref.shape[0] // KEYS, step, 0)
+    for p in pairs:
+        sums = total[p:p + 1]
+        mixed = acc[p] / sums
+        joined = jnp.concatenate([mixed[:HD, :QUERIES], mixed[HD:, QUERIES:]], axis=0)
+        out_ref[rows, p * 128:(p + 1) * 128] = joined.T.astype(BF)
+        sums_ref[i, p:p + 1] = top[p:p + 1] + jnp.log(sums)
+
+
+def attend_back_block(
+    i, q_ref, q_at, k_ref, k_at, v_at, grad_ref, out_ref, out_at, sums_ref, low, high, causal, dq_ref, dq_at, acc, acc_k, acc_v
+):
+    pairs = range(4)
+    rows = tile_rows(i, QUERIES)
+    least, limit = low[pl.ds(i, 1)], high[pl.ds(i, 1)]
+    queries, grads, fixes, sums = [], [], [], []
+    ones = jnp.ones((8, 128), BF)
+    for p in pairs:
+        queries.append(both_heads(q_ref[rows, q_at + p * 128:q_at + p * 128 + 128] * jnp.bfloat16(HD ** -0.5)))
+        grad = both_heads(grad_ref[rows, p * 128:(p + 1) * 128])
+        grads.append(grad)
+        out = out_ref[rows, out_at + p * 128:out_at + p * 128 + 128].astype(F32)
+        product = grad.astype(F32) * jnp.concatenate([out, out], axis=0)
+        coarse = product.astype(BF)
+        fine = (product - coarse.astype(F32)).astype(BF)
+        fixes.append((dot(ones, coarse, NT) + dot(ones, fine, NT))[:1])
+        sums.append(sums_ref[i, p:p + 1])
+    acc[...] = jnp.zeros_like(acc)
+
+    def step(j, _):
+        at = pl.multiple_of(j * KEYS, KEYS)
+        seen = allowed_keys(least, limit, at)
+        attend_back_step(queries, grads, fixes, sums, k_ref, k_at, v_at, pl.ds(at, KEYS), seen, acc, acc_k, acc_v)
+        return 0
+
+    lax.fori_loop(0, i // 2 + 1 if causal else k_ref.shape[0] // KEYS, step, 0)
+    for p in pairs:
+        mixed = acc[p] * (HD ** -0.5)
+        joined = jnp.concatenate([mixed[:HD, :QUERIES], mixed[HD:, QUERIES:]], axis=0)
+        dq_ref[rows, dq_at + p * 128:dq_at + p * 128 + 128] = joined.T.astype(BF)
+
+
+def reach(query_ids, key_ids):
+    low = jnp.zeros(query_ids.shape, F32)
+    high = jnp.zeros(query_ids.shape, F32)
+    for segment in range(16):
+        here = query_ids == segment
+        before = jnp.sum((key_ids < segment).astype(F32), axis=(0, 1), keepdims=True)
+        upto = jnp.sum((key_ids <= segment).astype(F32), axis=(0, 1), keepdims=True)
+        low = low + jnp.where(here, before, 0.0)
+        high = high + jnp.where(here, upto, 0.0)
+    return low.astype(jnp.int32), high.astype(jnp.int32)
+
+
+def project_out(net, att, weight, part, part_in):
+    swaps = []
+    for i in range(4):
+        part[i] = dot(att[i * 256:i * 256 + 256], weight[...], NN).astype(BF).reshape(2, 128, -1)
+        swaps.append(net.send(part.at[i], part_in.at[i], net.core))
+    return swaps
+
+
+def ahead_kernel(
+    x_in, mem_in, top_in, ids, bias, wq, wk, wv, wo, wcq, wck, wcv, wco, inner, outer,
+    gain1, shift1, bias_o, gain2, shift2, bias_c, gain3, shift3,
+    x_out, mem_out, top_out, n1_out, qkv_out, att1_out, sums1_out, h1_out, n2_out, q2_out, kv2_out, att2_out, sums2_out,
+    h2_out, n3_out, act_out, slope_out, wqkv_out, wo_out, wc_out, wco_out, wi_out, wu_out, reach_out,
+    rows_x, rows_mem, rows_top, row, mem, weights, weights2, wo_vm, wco_vm, wi, normed, qkv, att, part, part_in, part_in2,
+    hidden, queries, keys, act, slope, biases, all_ids, spans, sums1, sums2, acc, top, total, sems, local_sems,
+):
+    net = Net(sems, local_sems)
+    core, chip = net.core_index, net.chip
+    net.meet()
+    enter_x = row_in(net, x_in, rows_x, row)
+    next(enter_x)
+    mine = pl.ds(2 * core, 2)
+    ids_copies = [net.move(ids, all_ids.at[mine]), net.send(ids, all_ids.at[mine], net.core)]
+    bias_own = net.move(bias, biases.at[0])
+    bias_copies = [
+        net.send(bias, biases.at[1], net.first),
+        net.send(bias, biases.at[2], net.second),
+        net.send(bias, biases.at[3], net.corner),
+    ]
+
+    def gather_columns(weight, target, kind, flip):
+        slot = lambda s: target.at[:, kind * 512 + s * 128:kind * 512 + s * 128 + 128]
+        return Gather(net, half_columns(net, weight, 128), slot, flip)
+
+    def gather_rows_of(weight, target, flip):
+        return Gather(net, half_rows(net, weight, 128), lambda s: target.at[pl.ds(s * 128, 128)], flip)
+
+    def gather_inner(k):
+        own = inner.at[pl.ds(k * 512, 512), pl.ds(pl.multiple_of(core * 512, 512), 512)]
+        return Gather(net, own, lambda s: wi.at[pl.ds(k * 512, 512), s * 512:s * 512 + 512], k == 1)
+
+    def gather_outer(k):
+        own = outer.at[pl.ds(pl.multiple_of(core * 512 + k * 256, 256), 256)]
+        return Gather(net, own, lambda s: wu_out.at[pl.ds(s * 512 + k * 256, 256)], k == 1)
+
+    gather_q = gather_columns(wq, weights, 0, False)
+    gather_k = gather_columns(wk, weights, 1, True)
+    gather_v = gather_columns(wv, weights, 2, False)
+    next(enter_x)
+    enter_mem = row_in(net, mem_in, rows_mem, mem)
+    next(enter_mem)
+    gather_o = gather_rows_of(wo, wo_vm, True)
+    gather_q.relay()
+    gather_k.relay()
+    gather_v.relay()
+    next(enter_x)
+    next(enter_mem)
+    for _ in enter_x:
+        pass
+    net.move(row, x_out)
+
+    def norm_first(i, _):
+        normed[tile_rows(i)] = norm_forward(row[i].reshape(256, -1).astype(F32), gain1[...], shift1[...])
+        return 0
+
+    lax.fori_loop(0, 4, norm_first, 0)
+    n1_move = net.move(normed, n1_out)
+    gather_o.relay()
+    gather_ck = gather_columns(wck, weights2, 1, False)
+    gather_cv = gather_columns(wcv, weights2, 2, True)
+    net.moved(bias_own)
+    for copy in bias_copies:
+        copy.wait_recv()
+    for gather in (gather_q, gather_k, gather_v):
+        gather.finish()
+    net.move(weights, wqkv_out)
+
+    def project_first(i, _):
+        tokens = normed[tile_rows(i)]
+        for kind in range(3):
+            cut = slice(kind * 512, kind * 512 + 512)
+            value = dot(tokens, weights[:, cut], NN)
+            if kind != 1:
+                at = 0 if kind == 0 else 1
+                value = value + jnp.concatenate([biases[s, at:at + 1] for s in range(4)], axis=1)
+            qkv[tile_rows(i), cut] = value.astype(BF)
+        return 0
+
+    lax.fori_loop(0, 4, project_first, 0)
+    net.move(qkv, qkv_out)
+    net.moved(ids_copies[0])
+    ids_copies[1].wait_recv()
+    target_ids, source_ids = all_ids[chip, :8], all_ids[chip, 8:]
+    low, _ = reach(target_ids, target_ids)
+    spans[0] = low
+    place = lax.broadcasted_iota(jnp.int32, (8, 128), 0) * 128 + lax.broadcasted_iota(jnp.int32, (8, 128), 1)
+    spans[1] = place + 1
+    low, high = reach(target_ids, source_ids)
+    spans[2] = low
+    spans[3] = high
+    net.move(spans, reach_out)
+
+    def attend_first(i, _):
+        attend_block(i, qkv, 0, qkv, 512, 1024, spans.at[0], spans.at[1], True, att, sums1, acc, top, total)
+        return 0
+
+    lax.fori_loop(0, 4, attend_first, 0)
+    gather_ck.relay()
+    gather_cv.relay()
+    gather_cq = gather_columns(wcq, weights2, 0, False)
+    gather_co = gather_rows_of(wco, wco_vm, True)
+    next(enter_mem)
+    lax.fori_loop(4, 7, attend_first, 0)
+    gather_cq.relay()
+    gather_co.relay()
+    enter_top = row_in(net, top_in, rows_top, top_out)
+    next(enter_top)
+    for _ in enter_mem:
+        pass
+    net.move(mem, mem_out)
+    lax.fori_loop(7, 8, attend_first, 0)
+    att1_move = net.move(att, att1_out)
+    net.move(sums1, sums1_out)
+    next(enter_top)
+    gather_o.finish()
+    net.move(wo_vm, wo_out)
+    swaps = project_out(net, att, wo_vm, part, part_in)
+    inners = [gather_inner(0), gather_inner(1)]
+    for gather in (gather_ck, gather_cv):
+        gather.finish()
+    values_bias = jnp.concatenate([biases[s, 3:4] for s in range(4)], axis=1)
+    query_bias = jnp.concatenate([biases[s, 2:3] for s in range(4)], axis=1)
+
+    def project_memory(i, _):
+        tokens = mem[i].reshape(256, -1)
+        keys[tile_rows(i), :512] = dot(tokens, weights2[:, 512:1024], NN).astype(BF)
+        keys[tile_rows(i), 512:] = (dot(tokens, weights2[:, 1024:], NN) + values_bias).astype(BF)
+        return 0
+
+    lax.fori_loop(0, 4, project_memory, 0)
+    net.move(keys, kv2_out)
+    net.moved(n1_move)
+    for i in range(4):
+        swaps[i].wait_recv()
+
+    def middle_rows(i, _):
+        value = row[i].astype(F32) + part[i].astype(F32) + part_in[i].astype(F32)
+        value = value.reshape(256, -1) + bias_o[...]
+        hidden[tile_rows(i)] = value
+        normed[tile_rows(i)] = norm_forward(value, gain2[...], shift2[...])
+        return 0
+
+    lax.fori_loop(0, 4, middle_rows, 0)
+    h1_move = net.move(hidden, h1_out)
+    n2_move = net.move(normed, n2_out)
+    gather_cq.finish()
+    net.move(weights2, wc_out)
+
+    def project_query(i, _):
+        queries[tile_rows(i)] = (dot(normed[tile_rows(i)], weights2[:, :512], NN) + query_bias).astype(BF)
+        return 0
+
+    lax.fori_loop(0, 4, project_query, 0)
+    net.move(queries, q2_out)
+    net.moved(att1_move)
+    next(enter_top)
+    inners[0].relay()
+    inners[1].relay()
+    outers = [gather_outer(0), gather_outer(1)]
+
+    def attend_second(i, _):
+        attend_block(i, queries, 0, keys, 0, 512, spans.at[2], spans.at[3], False, att, sums2, acc, top, total)
+        return 0
+
+    lax.fori_loop(0, 4, attend_second, 0)
+    outers[0].relay()
+    outers[1].relay()
+    for _ in enter_top:
+        pass
+    lax.fori_loop(4, 8, attend_second, 0)
+    net.move(att, att2_out)
+    net.move(sums2, sums2_out)
+    gather_co.finish()
+    net.move(wco_vm, wco_out)
+    for copy in swaps:
+        net.sent(copy)
+    swaps = project_out(net, att, wco_vm, part, part_in2)
+    net.moved(h1_move)
+    net.moved(n2_move)
+    for i in range(4):
+        swaps[i].wait_recv()
+
+    def last_rows(i, _):
+        value = part[i].astype(F32) + part_in2[i].astype(F32)
+        value = hidden[tile_rows(i)] + value.reshape(256, -1) + bias_c[...]
+        hidden[tile_rows(i)] = value
+        normed[tile_rows(i)] = norm_forward(value, gain3[...], shift3[...])
+        return 0
+
+    lax.fori_loop(0, 4, last_rows, 0)
+    net.move(hidden, h2_out)
+    net.move(normed, n3_out)
+    inners[0].finish()
+    inners[1].finish()
+    net.move(wi, wi_out)
+
+    def feed(i, _):
+        tokens = normed[tile_rows(i)]
+        for s in range(4):
+            cut = slice(s * 512, s * 512 + 512)
+            unit_bias = jnp.concatenate([biases[s, 4 + k:5 + k] for k in range(4)], axis=1)
+            pre = dot(tokens, wi[:, cut], NN) + unit_bias
+            sigmoid = jax.nn.sigmoid(pre)
+            act[tile_rows(i), cut] = (pre * sigmoid).astype(BF)
+            slope[tile_rows(i), cut] = (sigmoid * (1.0 + pre * (1.0 - sigmoid))).astype(BF)
+        return 0
+
+    lax.fori_loop(0, 4, feed, 0)
+    net.move(act, act_out)
+    net.move(slope, slope_out)
+    for gather in outers:
+        gather.finish()
+    net.finish()
+
+
+def ahead(x, mem, top, ids, bias, weights, vectors):
+    length, width = 1024, x.shape[-1]
+    shape = jax.ShapeDtypeStruct
+    quarters = (4, 2, 128, width)
+    rows = lambda columns, kind=BF: shape((length, columns), kind)
+    sums = shape((8, 4, 256), F32)
+    return call_remote(
+        ahead_kernel, 1,
+        [a.reshape(2, 2, -1, width) for a in (x, mem, top)] + [ids, bias] + list(weights) + [v[None] for v in vectors],
+        [ANY] * 15 + [VM] * 8,
+        [
+            shape(quarters, BF), shape(quarters, BF), shape(quarters, BF), rows(width), rows(1536), rows(512), sums,
+            rows(width, F32), rows(width), rows(512), rows(1024), rows(512), sums,
+            rows(width, F32), rows(width), rows(2048), rows(2048),
+            shape((width, 1536), BF), shape((512, width), BF), shape((width, 1536), BF), shape((512, width), BF),
+            shape((width, 2048), BF), shape((2048, width), BF), shape((4, 8, 128), jnp.int32),
+        ],
+        [ANY] * 24,
+        [pltpu.VMEM((4, 128, width), BF)] * 3 + [pltpu.VMEM(quarters, BF)] * 2 + [pltpu.VMEM((width, 1536), BF)] * 2
+        + [pltpu.VMEM((512, width), BF)] * 2
+        + [
+            pltpu.VMEM((width, 2048), BF), pltpu.VMEM((length, width), BF), pltpu.VMEM((length, 1536), BF),
+            pltpu.VMEM((length, 512), BF), pltpu.VMEM(quarters, BF), pltpu.VMEM(quarters, BF), pltpu.VMEM(quarters, BF),
+            pltpu.VMEM((length, width), F32), pltpu.VMEM((length, 512), BF), pltpu.VMEM((length, 1024), BF),
+            pltpu.VMEM((length, 2048), BF), pltpu.VMEM((length, 2048), BF), pltpu.VMEM((4, 8, 128), F32),
+            pltpu.VMEM((4, 16, 128), jnp.int32), pltpu.VMEM((4, 8, 128), jnp.int32),
+            pltpu.VMEM((8, 4, 256), F32), pltpu.VMEM((8, 4, 256), F32),
+            pltpu.VMEM((4, 128, 256), F32), pltpu.VMEM((4, 256), F32), pltpu.VMEM((4, 256), F32),
+        ],
+        vmem=62, name="ahead",
+    )
+
+
+def turn_kernel(
+    act_in, slope_in, n3_in, h2_in, top_in, wi_in, wu_in, wco_in, q_in, kv_in, att_in, sums_in, reach_in, gain, bias_u,
+    block_out, gh_out, outer_out, inner_out, heads_out, vectors_out, split_out,
+    act, slope, wu, wi, g_outer, g_inner, hidden, row, normed, wco, part, back_in, out_part, out_in, gatt,
+    pieces, rows_back, acc_k, acc_v, acc, spans, sums, vectors, split, *rest,
+):
+    lands, (sems, local_sems) = rest[:-2], rest[-2:]
+    net = Net(sems, local_sems)
+    core = net.core_index
+    loads = [
+        net.move(source, target)
+        for source, target in (
+            (act_in, act), (top_in, row), (wu_in, wu), (slope_in, slope), (n3_in, normed), (wi_in, wi), (h2_in, hidden),
+            (wco_in, wco), (reach_in, spans), (sums_in, sums),
+        )
+    ]
+    net.meet()
+    whole_row = lambda: row[...].reshape(1024, -1)
+    outers = [
+        Scatter(net, lambda s, k=k: g_outer.at[pl.ds(s * 512 + k * 256, 256)], 1 + k, lands[k * 3:k * 3 + 3])
+        for k in range(2)
+    ]
+    outer_lines = [
+        Line(
+            net, g_outer.at[pl.ds(k * 256, 256)], lands[12 + k * 2:14 + k * 2],
+            lambda c, h, k=k: outer_out.at[pl.ds(pl.multiple_of(c * 512 + k * 256 + h * 128, 128), 128)],
+        )
+        for k in range(2)
+    ]
+    inners = [
+        Scatter(
+            net, lambda s, k=k: g_inner.at[pl.ds(k * 512, 512), s * 512:s * 512 + 512], 1 + k,
+            lands[6 + k * 3:9 + k * 3],
+        )
+        for k in range(2)
+    ]
+
+    def outer_grad(k, s):
+        weight_grad(lambda cut: act[:, cut], whole_row, g_outer, s * 512 + k * 256, 256)
+
+    def inner_grad(k, s):
+        cut = slice(s * 512, s * 512 + 512)
+        weight_grad(lambda rows: normed[:, rows], lambda: slope[:, cut], g_inner, k * 512, 512, cut)
+
+    net.moved(loads[0])
+    net.moved(loads[1])
+    for k in range(2):
+        outer_grad(k, 3)
+        outer_grad(k, 1 + k)
+        outers[k].start()
+    for k in range(2):
+        outer_grad(k, 2 - k)
+        outer_grad(k, 0)
+    for copy in loads[2:]:
+        net.moved(copy)
+    split[...] = jnp.zeros_like(split)
+    vectors[...] = jnp.zeros_like(vectors)
+
+    def feed_back(i, _):
+        tokens = row[i].reshape(256, -1)
+        for s in range(4):
+            cut = slice(s * 512, s * 512 + 512)
+            value = (dot(tokens, wu[cut], NT) * slope[tile_rows(i), cut].astype(F32)).astype(BF)
+            slope[tile_rows(i), cut] = value
+            split[0:1, cut] += jnp.sum(value.astype(F32), axis=0, keepdims=True)
+        return 0
+
+    lax.fori_loop(0, 4, feed_back, 0)
+    swaps = []
+    for i in range(4):
+        value = dot(slope[i * 256:i * 256 + 256], wi[...], NT)
+        part[i] = value.astype(BF).reshape(2, 128, -1)
+        swaps.append(net.send(part.at[i], back_in.at[i], net.core))
+    for k in range(2):
+        inner_grad(k, 3)
+        inner_grad(k, 1 + k)
+        inners[k].start()
+    outers[0].middle()
+    outers[1].middle()
+    for copy in swaps:
+        copy.wait_recv()
+
+    def feed_out(i, _):
+        out_part[i] = dot(act[tile_rows(i)], wu[...], NN).astype(BF).reshape(2, 128, -1)
+        return 0
+
+    lax.fori_loop(0, 4, feed_out, 0)
+    out_swap = net.send(out_part.at[:, 1 - core], out_in, net.core)
+    loads = [
+        net.move(kv_in, act.at[:, :1024]), net.move(q_in, act.at[:, 1024:1536]), net.move(att_in, act.at[:, 1536:]),
+    ]
+    for k in range(2):
+        inner_grad(k, 2 - k)
+        inner_grad(k, 0)
+    out_swap.wait_recv()
+    for i in range(4):
+        pieces[i] = (hidden[i, core] + out_part[i, core].astype(F32) + out_in[i].astype(F32) + bias_u[...]).astype(BF)
+    leave = row_out(net, pieces, rows_back, block_out)
+    next(leave)
+
+    def back(i, _):
+        grad = (part[i].astype(F32) + back_in[i].astype(F32)).reshape(256, -1)
+        change, by_gain, by_shift = norm_back_tile(grad, hidden[i].reshape(256, -1), gain[...])
+        top = row[i].reshape(256, -1).astype(F32)
+        value = top + change
+        hidden[i] = value.reshape(2, 128, -1)
+        gatt[tile_rows(i)] = dot(value.astype(BF), wco[...], NT).astype(BF)
+        vectors[4:5] += by_gain
+        vectors[5:6] += by_shift
+        vectors[6:7] += jnp.sum(top, axis=0, keepdims=True)
+        vectors[3:4] += jnp.sum(value, axis=0, keepdims=True)
+        return 0
+
+    lax.fori_loop(0, 4, back, 0)
+    net.move(hidden, gh_out)
+    net.move(vectors, vectors_out)
+    net.move(split, split_out)
+    outers[0].own()
+    outer_lines[0].line0()
+    outers[1].own()
+    outer_lines[1].line0()
+    inners[0].middle()
+    inners[1].middle()
+    for copy in loads:
+        net.moved(copy)
+    acc_k[...] = jnp.zeros_like(acc_k)
+    acc_v[...] = jnp.zeros_like(acc_v)
+
+    def attend_back(i, _):
+        attend_back_block(
+            i, act, 1024, act, 0, 512, gatt, act, 1536, sums, spans.at[2], spans.at[3], False, slope, 0, acc, acc_k, acc_v
+        )
+        return 0
+
+    lax.fori_loop(0, 3, attend_back, 0)
+    outer_lines[0].line1()
+    outer_lines[1].line1()
+    next(leave)
+    lax.fori_loop(3, 6, attend_back, 0)
+    outer_lines[0].line2()
+    outer_lines[1].line2()
+    inners[0].own()
+    net.move(g_inner.at[pl.ds(0, 512), :512], inner_out.at[pl.ds(0, 512)])
+    inners[1].own()
+    net.move(g_inner.at[pl.ds(512, 512), :512], inner_out.at[pl.ds(512, 512)])
+    lax.fori_loop(6, 8, attend_back, 0)
+    slope[:, 512:1024] = acc_k[...].astype(BF)
+    slope[:, 1024:1536] = acc_v[...].astype(BF)
+    net.move(slope.at[:, :1536], heads_out)
+    outer_lines[0].line3()
+    outer_lines[1].line3()
+    for line in outer_lines:
+        line.end()
+    for _ in leave:
+        pass
+    net.finish()
+
+
+def turn(act, slope, n3, h2, top, wi, wu, wco, q, kv, att, sums, reach_rows, gain, bias_u):
+    length, width = act.shape[0], n3.shape[-1]
+    shape = jax.ShapeDtypeStruct
+    quarters = (4, 2, 128, width)
+    return call_remote(
+        turn_kernel, 2,
+        (
+            act, slope, n3, h2.reshape(quarters), top, wi, wu, wco, q, kv, att, sums, reach_rows, gain[None], bias_u[None],
+        ),
+        [ANY] * 13 + [VM] * 2,
+        [
+            shape((2, 2, 128, width), BF), shape(quarters, F32), shape((1024, width), BF), shape((width, 512), BF),
+            shape((length, 1536), BF), shape((8, width), F32), shape((8, 2048), F32),
+        ],
+        [ANY] * 7,
+        [
+            pltpu.VMEM((length, 2048), BF), pltpu.VMEM((length, 2048), BF), pltpu.VMEM((2048, width), BF),
+            pltpu.VMEM((width, 2048), BF), pltpu.VMEM((2048, width), BF), pltpu.VMEM((width, 2048), BF),
+            pltpu.VMEM(quarters, F32), pltpu.VMEM(quarters, BF), pltpu.VMEM((length, width), BF),
+            pltpu.VMEM((512, width), BF), pltpu.VMEM(quarters, BF), pltpu.VMEM(quarters, BF), pltpu.VMEM(quarters, BF),
+            pltpu.VMEM((4, 128, width), BF), pltpu.VMEM((length, 512), BF),
+            pltpu.VMEM((4, 128, width), BF), pltpu.VMEM((4, 128, width), BF),
+            pltpu.VMEM((length, 512), F32), pltpu.VMEM((length, 512), F32), pltpu.VMEM((4, 128, 256), F32),
+            pltpu.VMEM((4, 8, 128), jnp.int32), pltpu.VMEM((8, 4, 256), F32),
+            pltpu.VMEM((8, width), F32), pltpu.VMEM((8, 2048), F32),
+        ]
+        + landing(256, width) * 2 + landing(512, 512) * 2 + line_landing(256, width) * 2,
+        vmem=62, name="turn",
+    )
+
+
+def last_kernel(
+    heads_in, n2_in, mem_in, att2_in, gh_in, h1_in, wc_in, wo_in, inner_in, qkv_in, att1_in, sums_in, reach_in, n1_in, x_in,
+    wqkv_in, shared_in, split_in, gain2, gain1,
+    mem_out, grad_out, cross_out, cross_o_out, heads_out, o_out, inner_out, shared_out, late_out, split_out,
+    dqkv, normed, tokens, att, grads, hidden, weights, wo, part, part_in, mem_part, mem_back, grad_in,
+    pieces_mem, rows_mem, pieces, rows_back, g_cross, g_cross_o, g_heads, g_o, gatt, acc, spans, sums,
+    inner_total,
+    shared, shared_land, late, late_land, split, split_land, split_full, *rest,
+):
+    lands, (sems, local_sems) = rest[:-2], rest[-2:]
+    net = Net(sems, local_sems)
+    core, chip = net.core_index, net.chip
+    place = lax.axis_index("dp")
+    loads = [
+        net.move(source, target)
+        for source, target in (
+            (heads_in, dqkv), (wc_in, weights), (inner_in, inner_total), (mem_in, tokens), (n2_in, normed), (att2_in, att),
+            (gh_in, grads), (h1_in, hidden), (wo_in, wo), (reach_in, spans), (sums_in, sums), (shared_in, shared),
+            (split_in, split),
+        )
+    ]
+    net.meet()
+    inner_lines = [
+        Line(
+            net, inner_total.at[pl.ds(k * 512, 512)], lands[40 + k * 2:42 + k * 2],
+            lambda c, h, k=k: inner_out.at[
+                pl.ds(pl.multiple_of(k * 512 + h * 256, 256), 256), pl.ds(pl.multiple_of(c * 512, 512), 512)
+            ],
+        )
+        for k in range(2)
+    ]
+    scatters = head_scatters(net, g_cross, g_cross_o, lands[:12])
+    lines = head_lines(
+        net, lambda kind: g_cross.at[:, kind * 512:kind * 512 + 128], g_cross_o.at[pl.ds(0, 128)], cross_out,
+        cross_o_out, lands[12:20],
+    )
+    for copy in loads[:3]:
+        net.moved(copy)
+    inner_lines[0].line0()
+    inner_lines[1].line0()
+    swaps = []
+    for i in range(4):
+        value = dot(dqkv[i * 256:i * 256 + 256, :512], weights[:, :512], NT)
+        part[i] = value.astype(BF).reshape(2, 128, -1)
+        swaps.append(net.send(part.at[i], part_in.at[i], net.core))
+    for copy in loads[3:]:
+        net.moved(copy)
+    memory = lambda cut: tokens[:, :, :, cut].reshape(1024, -1)
+    for kind in (1, 2):
+        cut = slice(kind * 512, kind * 512 + 512)
+        weight_grad(memory, lambda: dqkv[:, cut], g_cross, 0, 1024, cut)
+        scatters[kind].start()
+
+    def memory_back(i, _):
+        rows = tile_rows(i)
+        value = dot(dqkv[rows, 512:1024], weights[:, 512:1024], NT) + dot(dqkv[rows, 1024:], weights[:, 1024:], NT)
+        mem_part[i] = value.astype(BF).reshape(2, 128, -1)
+        return 0
+
+    lax.fori_loop(0, 4, memory_back, 0)
+    mem_swap = net.send(mem_part.at[:, 1 - core], mem_back, net.core)
+    load_qkv = net.move(qkv_in, weights)
+    load_x = net.move(x_in, tokens)
+    weight_grad(lambda cut: normed[:, cut], lambda: dqkv[:, :512], g_cross, 0, 1024, slice(0, 512))
+    load_n1 = net.move(n1_in, normed)
+    weight_grad(lambda cut: att[:, cut], lambda: grads[...].reshape(1024, -1).astype(BF), g_cross_o, 0, 512)
+    load_att = net.move(att1_in, att)
+    for at, kind in ((2, 0), (3, 2)):
+        total = jnp.sum(dqkv[:, kind * 512:kind * 512 + 512].astype(F32), axis=0, keepdims=True)
+        for s in range(4):
+            split[s, at:at + 1] = total[:, s * 128:s * 128 + 128]
+    for copy in swaps:
+        copy.wait_recv()
+
+    def back(i, _):
+        grad = (part[i].astype(F32) + part_in[i].astype(F32)).reshape(256, -1)
+        change, by_gain, by_shift = norm_back_tile(grad, hidden[tile_rows(i)], gain2[...])
+        value = grads[i].reshape(256, -1) + change
+        grads[i] = value.reshape(2, 128, -1)
+        gatt[tile_rows(i)] = dot(value.astype(BF), wo[...], NT).astype(BF)
+        shared[1:2] += by_gain
+        shared[2:3] += by_shift
+        shared[0:1] += jnp.sum(value, axis=0, keepdims=True)
+        return 0
+
+    lax.fori_loop(0, 4, back, 0)
+    scatters[1].middle()
+    scatters[2].middle()
+    scatters[0].start()
+    scatters[3].start()
+    mem_swap.wait_recv()
+    for i in range(4):
+        pieces_mem[i] = (mem_part[i, core].astype(F32) + mem_back[i].astype(F32)).astype(BF)
+    leave_mem = row_out(net, pieces_mem, rows_mem, mem_out)
+    next(leave_mem)
+    inner_lines[0].line1()
+    inner_lines[1].line1()
+    stages = [(place, net.chips[0]), (place, net.chips[1]), net.near_plane, net.far_plane]
+    shared_copy = net.send(shared, shared_land.at[0], stages[0])
+
+    def shared_stage(at):
+        nonlocal shared_copy
+        shared_copy.wait_recv()
+        net.sent(shared_copy)
+        shared[...] += shared_land[at]
+        if at < 3:
+            shared_copy = net.send(shared, shared_land.at[at + 1], stages[at + 1])
+
+    hidden[...] = jnp.zeros_like(hidden)
+    for copy in (load_qkv, load_att):
+        net.moved(copy)
+
+    def attend_back(i, _):
+        attend_back_block(
+            i, weights, 0, weights, 512, 1024, gatt, att, 0, sums, spans.at[0], spans.at[1], True, dqkv, 0, acc,
+            hidden.at[:, :512], hidden.at[:, 512:],
+        )
+        return 0
+
+    lax.fori_loop(0, 4, attend_back, 0)
+    scatters[1].own()
+    lines[1].line0()
+    scatters[2].own()
+    lines[2].line0()
+    scatters[0].middle()
+    scatters[3].middle()
+    inner_lines[0].line2()
+    inner_lines[1].line2()
+    next(leave_mem)
+    shared_stage(0)
+    lax.fori_loop(4, 6, attend_back, 0)
+    lines[1].line1()
+    lines[2].line1()
+    scatters[0].own()
+    scatters[3].own()
+    lines[0].line0()
+    lines[3].line0()
+    inner_lines[0].line3()
+    inner_lines[1].line3()
+    shared_stage(1)
+    lax.fori_loop(6, 8, attend_back, 0)
+    load_w = net.move(wqkv_in, weights)
+    dqkv[:, 512:] = hidden[...].astype(BF)
+    lines[1].line2()
+    lines[2].line2()
+    lines[0].line1()
+    lines[3].line1()
+    shared_stage(2)
+    for copy in (load_n1, load_x):
+        net.moved(copy)
+    own_scatters = head_scatters(net, g_heads, g_o, lands[20:32])
+    own_lines = head_lines(
+        net, lambda kind: g_heads.at[:, kind * 512:kind * 512 + 128], g_o.at[pl.ds(0, 128)], heads_out, o_out,
+        lands[32:40],
+    )
+
+    def head_grad(kind):
+        cut = slice(kind * 512, kind * 512 + 512)
+        weight_grad(lambda rows: normed[:, rows], lambda: dqkv[:, cut], g_heads, 0, 1024, cut)
+
+    head_grad(0)
+    own_scatters[0].start()
+    head_grad(2)
+    own_scatters[2].start()
+    net.moved(load_w)
+    for copy in swaps:
+        net.sent(copy)
+
+    def first_back(i, _):
+        part[i] = dot(dqkv[tile_rows(i)], weights[...], NT).astype(BF).reshape(2, 128, -1)
+        return 0
+
+    lax.fori_loop(0, 4, first_back, 0)
+    swap = net.send(part.at[:, 1 - core], grad_in, net.core)
+    head_grad(1)
+    weight_grad(lambda cut: att[:, cut], lambda: grads[...].reshape(1024, -1).astype(BF), g_o, 0, 512)
+    own_scatters[0].middle()
+    own_scatters[2].middle()
+    own_scatters[1].start()
+    own_scatters[3].start()
+    lines[1].line3()
+    lines[2].line3()
+    lines[0].line2()
+    lines[3].line2()
+    shared_stage(3)
+    for at, kind in ((0, 0), (1, 2)):
+        total = jnp.sum(dqkv[:, kind * 512:kind * 512 + 512].astype(F32), axis=0, keepdims=True)
+        for s in range(4):
+            split[s, at:at + 1] = total[:, s * 128:s * 128 + 128]
+    split_copies = [
+        net.send(split.at[s], split_land.at[s - 1], device)
+        for s, device in ((1, net.first), (2, net.second), (3, net.corner))
+    ]
+    swap.wait_recv()
+    late[...] = jnp.zeros_like(late)
+    for i in range(4):
+        grad = part[i, core].astype(F32) + grad_in[i].astype(F32)
+        change, by_gain, by_shift = norm_back_tile(grad, tokens[i, core].astype(F32), gain1[...])
+        pieces[i] = (grads[i, core] + change).astype(BF)
+        late[0:1] += by_gain
+        late[1:2] += by_shift
+    late_copy = net.send(late, late_land.at[0], net.core)
+    leave = row_out(net, pieces, rows_back, grad_out)
+
+    def late_stage(at):
+        nonlocal late_copy
+        late_copy.wait_recv()
+        net.sent(late_copy)
+        late[...] += late_land[at]
+        if at < 4:
+            late_copy = net.send(late, late_land.at[at + 1], stages[at])
+
+    def split_stage(at):
+        nonlocal split_copies
+        for copy in split_copies:
+            copy.wait_recv()
+            net.sent(copy)
+        if at == 0:
+            split[0] = split[0] + split_land[0] + split_land[1] + split_land[2]
+        else:
+            split[0] = split[0] + split_land[2 + at]
+        if at < 2:
+            device = (net.near_plane, net.far_plane)[at]
+            split_copies = [net.send(split.at[0], split_land.at[3 + at], device)]
+        else:
+            split_full[core] = split[0]
+            split_copies = [net.send(split_full.at[core], split_full.at[core], net.core)]
+
+    own_scatters[0].own()
+    own_lines[0].line0()
+    own_scatters[2].own()
+    own_lines[2].line0()
+    lines[0].line3()
+    lines[3].line3()
+    late_stage(0)
+    split_stage(0)
+    own_scatters[1].middle()
+    own_scatters[3].middle()
+    next(leave)
+    late_stage(1)
+    own_lines[0].line1()
+    own_lines[2].line1()
+    split_stage(1)
+    late_stage(2)
+    own_scatters[1].own()
+    own_lines[1].line0()
+    own_scatters[3].own()
+    own_lines[3].line0()
+    own_lines[0].line2()
+    own_lines[2].line2()
+    late_stage(3)
+    split_stage(2)
+    own_lines[1].line1()
+    own_lines[3].line1()
+    next(leave)
+    late_stage(4)
+    own_lines[0].line3()
+    own_lines[2].line3()
+    own_lines[1].line2()
+    own_lines[3].line2()
+    own_lines[1].line3()
+    own_lines[3].line3()
+    for line in inner_lines + lines + own_lines:
+        line.end()
+    for _ in leave_mem:
+        pass
+    for _ in leave:
+        pass
+    split_copies[0].wait_recv()
+    for source, target in (
+        (shared, shared_out), (late, late_out), (split_full, split_out),
+    ):
+        net.move(source, target)
+    net.finish()
+
+
+def last(heads, n2, mem, att2, gh, h1, wc, wo, inner_total, qkv, att1, sums, reach_rows, n1, x, wqkv, shared, split, gain2, gain1):
+    length, width = heads.shape[0], n1.shape[-1]
+    shape = jax.ShapeDtypeStruct
+    quarters = (4, 2, 128, width)
+    own = [shape((3, width, 256), BF), shape((256, width), BF)]
+    return call_remote(
+        last_kernel, 3,
+        (
+            heads, n2, mem, att2, gh, h1, wc, wo, inner_total, qkv, att1, sums, reach_rows, n1, x, wqkv, shared, split,
+            gain2[None], gain1[None],
+        ),
+        [ANY] * 18 + [VM] * 2,
+        [shape((2, 2, 128, width), BF)] * 2 + own + own
+        + [shape((width, 1024), BF), shape((8, width), F32), shape((8, width), F32), shape((2, 8, 128), F32)],
+        [ANY] * 10,
+        [
+            pltpu.VMEM((length, 1536), BF), pltpu.VMEM((length, width), BF), pltpu.VMEM(quarters, BF),
+            pltpu.VMEM((length, 512), BF), pltpu.VMEM(quarters, F32), pltpu.VMEM((length, width), F32),
+            pltpu.VMEM((width, 1536), BF), pltpu.VMEM((512, width), BF), pltpu.VMEM(quarters, BF),
+            pltpu.VMEM(quarters, BF), pltpu.VMEM(quarters, BF), pltpu.VMEM((4, 128, width), BF),
+            pltpu.VMEM((4, 128, width), BF),
+        ]
+        + [pltpu.VMEM((4, 128, width), BF)] * 4
+        + [pltpu.VMEM((width, 1536), BF), pltpu.VMEM((512, width), BF)] * 2
+        + [
+            pltpu.VMEM((length, 512), BF), pltpu.VMEM((4, 128, 256), F32), pltpu.VMEM((4, 8, 128), jnp.int32),
+            pltpu.VMEM((8, 4, 256), F32), pltpu.VMEM((width, 512), BF),
+        ]
+        + [
+            pltpu.VMEM((8, width), F32), pltpu.VMEM((4, 8, width), F32),
+            pltpu.VMEM((8, width), F32), pltpu.VMEM((5, 8, width), F32),
+            pltpu.VMEM((4, 8, 128), F32), pltpu.VMEM((5, 8, 128), F32), pltpu.VMEM((2, 8, 128), F32),
+        ]
+        + (head_landing(width) + head_line_landing(width)) * 2 + line_landing(512, 512) * 2,
+        vmem=63, name="last",
+    )
+
+
+def solution(mesh):
+    if mesh.shape["tensor"] != 4 or mesh.shape["dp"] != 8:
+        return general_solution(mesh)
+
+    def local(
+        layer_input, memory, grad_out, target_segments, source_segments,
+        self_gain, self_shift, query_weight, query_bias, key_weight, value_weight, value_bias,
+        attend_weight, attend_bias,
+        cross_gain, cross_shift, cross_query, cross_query_bias, cross_key, cross_value, cross_value_bias,
+        cross_attend, cross_attend_bias,
+        feed_gain, feed_shift, inner_weight, inner_bias, outer_weight, outer_bias,
+    ):
+        core = lax.axis_index("dp") % 2
+        half = lambda b: lax.dynamic_slice_in_dim(b, core * (b.shape[0] // 2), b.shape[0] // 2)
+        ids = jnp.stack([target_segments, source_segments], axis=1).reshape(2, 16, 128)
+        biases = jnp.concatenate([half(b) for b in (query_bias, value_bias, cross_query_bias, cross_value_bias, inner_bias)])
+        (
+            x, mem, top, n1, qkv1, att1, sums1, h1, n2, q2, kv2, att2, sums2, h2, n3, act, slope,
+            wqkv, wo, wc, wco, wi, wu, spans,
+        ) = ahead(
+            layer_input, memory, grad_out, ids, biases.reshape(8, 128),
+            (
+                query_weight, key_weight, value_weight, attend_weight, cross_query, cross_key, cross_value, cross_attend,
+                inner_weight, outer_weight,
+            ),
+            (self_gain, self_shift, attend_bias, cross_gain, cross_shift, cross_attend_bias, feed_gain, feed_shift),
+        )
+        block_out, gh2, f_outer, f_inner, heads2, shared, split = turn(
+            act, slope, n3, h2, top, wi, wu, wco, q2, kv2, att2, sums2, spans, feed_gain, outer_bias
+        )
+        split = jnp.concatenate([jnp.zeros((4, 4, 128), F32), split[0].reshape(4, 4, 128)], axis=1)
+        memory_grad, input_grad, c_heads, c_out, s_heads, s_out, f_inner, shared, late, split = last(
+            heads2, n2, mem, att2, gh2, h1, wc, wo, f_inner, qkv1, att1, sums1, spans, n1, x, wqkv, shared, split,
+            cross_gain, self_gain,
+        )
+        split_of = lambda at, rows: split[:, at:at + rows].reshape(-1)
+        tokens = layer_input.shape
+        return (
+            block_out.reshape(tokens), input_grad.reshape(tokens).astype(F32), memory_grad.reshape(tokens).astype(F32),
+            late[0], late[1],
+            s_heads[0].astype(F32), split_of(0, 1), s_heads[1].astype(F32), s_heads[2].astype(F32), split_of(1, 1),
+            s_out.astype(F32), shared[0],
+            shared[1], shared[2],
+            c_heads[0].astype(F32), split_of(2, 1), c_heads[1].astype(F32), c_heads[2].astype(F32), split_of(3, 1),
+            c_out.astype(F32), shared[3],
+            shared[4], shared[5],
+            f_inner.astype(F32), split_of(4, 4), f_outer.astype(F32), shared[6],
+        )
+
+    row, one, by_column, by_row = P("dp", "tensor", None), P(), P(None, "tensor"), P("tensor", None)
+    part, ids = P("tensor"), P("dp", None)
+    return jax.shard_map(
+        local,
+        mesh=mesh,
+        in_specs=(
+            row, row, row, ids, ids,
+            one, one, by_column, part, by_column, by_column, part, by_row, one,
+            one, one, by_column, part, by_column, by_column, part, by_row, one,
+            one, one, by_column, part, by_row, one,
+        ),
+        out_specs=(
+            row, row, row,
+            one, one, by_column, part, by_column, by_column, part, by_row, one,
+            one, one, by_column, part, by_column, by_column, part, by_row, one,
+            one, one, by_column, part, by_row, one,
+        ),
+        check_vma=False,
+    )
+
+
 BLOCK_ROWS = 512
 
 
-def norm_forward(values, gain, shift):
+def general_norm_forward(values, gain, shift):
     average = jnp.mean(values, axis=-1, keepdims=True)
     center = values - average
     inverse = lax.rsqrt(jnp.mean(center * center, axis=-1, keepdims=True) + EPSILON)
@@ -19,7 +1284,7 @@
     return ((normed * gain + shift).astype(jnp.bfloat16), normed, inverse)
 
 
-def norm_backward(grad_in, normed, inverse, gain):
+def general_norm_backward(grad_in, normed, inverse, gain):
     scaled = grad_in * gain
     first_mean = jnp.mean(scaled, axis=-1, keepdims=True)
     second_mean = jnp.mean(scaled * normed, axis=-1, keepdims=True)
@@ -44,7 +1309,7 @@
 
 
 def next_rows(values, gain, shift):
-    return gather_rows(norm_forward(values, gain, shift)[0])
+    return gather_rows(general_norm_forward(values, gain, shift)[0])
 
 
 def backward_rows(normed_low):
@@ -199,7 +1464,7 @@
     )
 
 
-def local(
+def general_local(
     layer_input,
     memory,
     grad_out,
@@ -259,7 +1524,7 @@
         )
     )
     grad_top = grad_out.astype(jnp.float32)
-    normed_low3, unit_third, inverse_third = norm_forward(kept_second, feed_gain, feed_shift)
+    normed_low3, unit_third, inverse_third = general_norm_forward(kept_second, feed_gain, feed_shift)
     rows_back3 = backward_rows(normed_low3)
     pre_back = project(rows_back3, inner_weight) + inner_bias
     sigmoid_back = jax.nn.sigmoid(pre_back)
@@ -274,11 +1539,11 @@
     grad_inner_weight = outer_sum(rows_back3, grad_inner)
     grad_inner_bias = bias_sum(grad_inner)
     grad_norm3 = reduce_inputs(project_back(grad_inner, inner_weight))
-    grad_from3, grad_feed_gain, grad_feed_shift = norm_backward(
+    grad_from3, grad_feed_gain, grad_feed_shift = general_norm_backward(
         grad_norm3, unit_third, inverse_third, feed_gain
     )
     grad_hidden2 = grad_top + grad_from3
-    normed_low2, unit_second, inverse_second = norm_forward(kept_first, cross_gain, cross_shift)
+    normed_low2, unit_second, inverse_second = general_norm_forward(kept_first, cross_gain, cross_shift)
     rows_back2 = backward_rows(normed_low2)
     query_back2 = (project(rows_back2, cross_query) + cross_query_bias).astype(jnp.bfloat16)
     keys_back2 = project(kept_memory, cross_key).astype(jnp.bfloat16)
@@ -311,11 +1576,11 @@
         tiled=True,
     ).astype(jnp.float32)
     grad_norm2 = reduce_inputs(project_back(grad_query2, cross_query))
-    grad_from2, grad_cross_gain, grad_cross_shift = norm_backward(
+    grad_from2, grad_cross_gain, grad_cross_shift = general_norm_backward(
         grad_norm2, unit_second, inverse_second, cross_gain
     )
     grad_hidden1 = grad_hidden2 + grad_from2
-    normed_low1, unit_first, inverse_first = norm_forward(kept_input, self_gain, self_shift)
+    normed_low1, unit_first, inverse_first = general_norm_forward(kept_input, self_gain, self_shift)
     rows_back1 = backward_rows(normed_low1)
     query_back1 = (project(rows_back1, query_weight) + query_bias).astype(jnp.bfloat16)
     keys_back1 = project(rows_back1, key_weight).astype(jnp.bfloat16)
@@ -344,7 +1609,7 @@
         + project_back(grad_keys1, key_weight)
         + project_back(grad_values1, value_weight)
     )
-    grad_from1, grad_self_gain, grad_self_shift = norm_backward(
+    grad_from1, grad_self_gain, grad_self_shift = general_norm_backward(
         grad_norm1, unit_first, inverse_first, self_gain
     )
     input_grad = grad_hidden1 + grad_from1
@@ -436,7 +1701,7 @@
     )
 
 
-def solution(mesh):
+def general_solution(mesh):
     placed = (
         P("dp", "tensor", None),
         P("dp", "tensor", None),
@@ -469,7 +1734,7 @@
         P(),
     )
     return jax.shard_map(
-        local,
+        general_local,
         mesh=mesh,
         in_specs=placed,
         out_specs=(

time: 1740 us -> 457 us (0.26)
  waiting for transfers between devices: 1040 us -> 0 us
  Pallas kernels: 0 us -> 420 us
  matrix products: 345 us -> 0 us
  other arithmetic: 144 us -> 15.3 us
  local copies, waits for them, and re-layouts: 89.4 us -> 12.1 us
  blocking collectives: 54.4 us -> 0 us
  loops' own time: 43.7 us -> 0 us
    reduce_scatter x7 -> x0, waiting for transfers between devices: 455 us -> none  [the longest x3 245 us: reduce_inputs(): lax.psum_scatter(partial_sum, 'tensor', scatter_dimension=1, tiled=True)]
    all_gather x10 -> x0, waiting for transfers between devices: 441 us -> none  [the longest x6 282 us: gather_rows(): return lax.all_gather(values, 'tensor', axis=1, tiled=True)]
    pallas_call x0 -> x3, Pallas kernels: none -> 420 us  [call_remote(): pl.pallas_call(kernel, in_specs=in_specs, out_specs=out_specs, out_shape=...]
    dot_general x100 -> x0, matrix products: 345 us -> none  [the longest x16 76 us: project(): jnp.einsum('rtd,dc->rtc', rows_in, weight, preferred_element_type=jnp.flo...]
    psum x1 -> x0, waiting for transfers between devices: 140 us -> none  [local(): lax.psum(grad_query_weight.astype(jnp.bfloat16), 'dp').astype(jnp.float32)]
    reduce_sum x28 -> x0, other arithmetic: 61 us -> none  [the longest x8 18.7 us: one_block(): row_total = jnp.sum(expo_scores, axis=-1, keepdims=True)]
    psum x2 -> x0, blocking collectives: 54.4 us -> none  [the longest x1 39.9 us: local(): lax.psum((grad_self_gain, grad_self_shift, grad_attend_bias, grad_cross_g...]
    convert_element_type x35 -> x6, other arithmetic: 64.6 us -> 14.6 us  [the longest x1 2.74 us: local(): c_heads[2].astype(F32)]
  transfers between devices with their start and end apart: 18 -> 0, of which waited for: 17 -> 0; matrix products, arithmetic and copies ran while one was open for 17% -> 0% of each run, Pallas kernels for 0% -> 0%
where the time goes in v2:
time: 457 us; the launch traced here: 449 us
  Pallas kernels  420 us (92%)
  other arithmetic  15.3 us (3%)
  local copies, waits for them, and re-layouts  12.1 us (3%)
    pallas_call x3, Pallas kernels, call_remote(): pl.pallas_call(kernel, in_specs=in_specs, out_specs=out_specs, out_shape=...  420 us

profile of v2, /device:TPU:1, one launch (start us, length us, event | category | flops | bytes accessed | tf_op | source)
XLA Modules:
  0.0 448.9 jit_solution(4715084332319556324)
XLA Ops:
  0.7 0.8 constant_dynamic-update-slice_fusion.4
  1.5 0.8 constant_dynamic-update-slice_fusion.3
  2.2 0.8 constant_dynamic-update-slice_fusion.2
  3.0 0.8 constant_dynamic-update-slice_fusion.1
  3.7 0.8 constant_dynamic-update-slice_fusion
  4.5 0.0 copy-start.7
  4.5 0.7 pad_add_fusion
  5.2 0.6 reshape.111.ids
  5.9 0.0 copy-done.7
  5.9 154.3 %ahead.1 = (bf16[4,2,128,1024]{3,2,1,0:T(8,128)(2,1)}, bf16[4,2,128,1024]{3,2,1,0:T(8,128)(2,1)}, bf16[4,2,128,1024]{3,2,1,0:T(8,128)(2,1)}, bf16[1024,1024]{1,0...) custom-call(bf16[2,2,128,1024]{3,2,1,0:T(8,128)(2,1)} %bitcast.58, ...), custom_call_target="tpu_custom_call" | custom-call | tf_op jit(solution)/shard_map/ahead/pallas_call | solution.py:224
  160.1 113.1 %turn.1 = (bf16[2,2,128,1024]{3,2,1,0:T(8,128)(2,1)}, f32[4,2,128,1024]{3,2,1,0:T(8,128)}, bf16[1024,1024]{1,0:T(8,128)(2,1)}, bf16[1024,512]{1,0:T(8,128)(2,1)}...) custom-call(bf16[1024,2048]{1,0:T(8,128)(2,1)} %get-tuple-element.68.act_in, ...), custom_call_target="tpu_custom_call" | custom-call | tf_op jit(solution)/shard_map/turn/pallas_call | solution.py:224
  273.2 0.8 slice.63
  274.0 0.6 concatenate.7.split_in
  274.7 153.0 %last.1 = (bf16[2,2,128,1024]{3,2,1,0:T(8,128)(2,1)}, bf16[2,2,128,1024]{3,2,1,0:T(8,128)(2,1)}, bf16[3,1024,256]{2,1,0:T(8,128)(2,1)}, bf16[256,1024]{1,0:T(8,1...) custom-call(bf16[1024,1536]{1,0:T(8,128)(2,1)} %get-tuple-element.82, ...), custom_call_target="tpu_custom_call" | custom-call | tf_op jit(solution)/shard_map/last/pallas_call | solution.py:224
  427.7 0.0 copy-start.5
  427.7 0.0 copy-start.6
  427.7 1.4 slice.82
  429.2 1.4 fusion.2
  430.6 1.8 fusion
  432.4 2.1 convert_element_type.70
  434.5 2.1 convert_element_type.77
  436.6 0.0 copy-done.5
  436.6 0.0 copy-done.6
  436.6 0.0 copy-start.1
  436.6 2.6 bitcast_convert_fusion
  439.2 0.0 copy-done.1
  439.2 0.0 copy-start
  439.2 2.5 convert_element_type.78
  441.7 0.0 copy-done
  441.7 0.0 copy-start.2
  441.7 0.0 copy-start.3
  441.7 2.5 convert_element_type.79
  444.2 0.0 copy-done.2
  444.2 0.5 copy-done.3
  444.7 0.0 copy-start.4
  444.7 2.7 bitcast_convert_fusion.2
  447.5 0.0 copy-done.4
  447.5 1.0 copy.63
  (2 shorter events, 0.0 us)
Async XLA Ops:
  4.5 1.4 copy-start.7
  427.7 8.9 %copy-start.5 = (bf16[2,2,128,1024]{3,2,1,0:T(8,128)(2,1)S(1)}, bf16[2,2,128,1024]{3,2,1,0:T(8,128)(2,1)}, u32[]{:S(2)}) copy-start(bf16[2,2,128,1024]{3,2,1,0:T(8,128)(2,1)} %get-tuple-element.99) | copy-start | bytes 3145732
  427.7 8.9 %copy-start.6 = (bf16[2,2,128,1024]{3,2,1,0:T(8,128)(2,1)S(1)}, bf16[2,2,128,1024]{3,2,1,0:T(8,128)(2,1)}, u32[]{:S(2)}) copy-start(bf16[2,2,128,1024]{3,2,1,0:T(8,128)(2,1)} %get-tuple-element.98) | copy-start | bytes 3145732
  436.6 2.6 copy-start.1
  439.2 2.5 copy-start
  441.7 2.5 copy-start.2
  441.7 3.0 copy-start.3
  444.7 2.7 copy-start.4
